TPU v7x, 256 devices: a whole 4x4x8 slice. The times are simulated.
256 devices in a mesh: pair: 2 (over core), seq: 32 (over y, z), tensor: 4 (over x).
Axes of the slice: x: 4, y: 4, z: 8, core: 2. Of those that a mesh axis runs over, the one named last changes fastest.
Arguments:
- latents: bfloat16 [2, 1, 8192, 1152], P('pair', None, 'seq'), may hold values from -36 to 36
- noise: bfloat16 [2, 1, 8192, 1152], P('pair', None, 'seq'), may hold values from -4 to 4
- timesteps: int32 [2, 1], P('pair'), may hold values from 50 to 949
- ref_losses: float32 [2, 1], replicated, may hold values from 0.5 to 2.5
- weights: bfloat16 [1152, 2, 4, 1152], P(None, None, None, 'tensor'), may hold values from -2.7 to 2.7
Outputs:
- dpo_loss: float32 [], replicated
- weight_grads: float32 [1152, 2, 4, 1152], P(('pair', 'seq'), None, None, 'tensor')
All inputs are finite; a program needn't handle non-finite values.
Results may differ from a plain program's by a relative error of at most 0.02.
Values may be sent and summed in bfloat16 or wider, within the bound.
A program may use at most 128 MiB of HBM per device.

v0:
```python
import math

import jax
import jax.numpy as jnp
from jax import lax
from jax.sharding import PartitionSpec as P

POSITIONS = 256
HEAD_DIM = 72


beta_dpo = 0.5
norm_eps = 1e-06


def layer_norm(hidden):
    center = hidden - jnp.mean(hidden, axis=-1, keepdims=True)
    inv_std = lax.rsqrt(jnp.mean(center * center, axis=-1, keepdims=True) + norm_eps)
    return (center * inv_std, inv_std)


def norm_backward(grad_norm, normed, inv_std):
    mean_grad = jnp.mean(grad_norm, axis=-1, keepdims=True)
    mean_prod = jnp.mean(grad_norm * normed, axis=-1, keepdims=True)
    return inv_std * (grad_norm - mean_grad - normed * mean_prod)


def attend_forward(queries, keyset, valueset):
    factor = HEAD_DIM ** (-0.5)
    scores = (
        jnp.einsum("bqhc,bkhc->bhqk", queries, keyset, preferred_element_type=jnp.float32) * factor
    )
    soft_weights = jax.nn.softmax(scores, axis=-1)
    rounded = soft_weights.astype(jnp.bfloat16)
    return jnp.einsum(
        "bhqk,bkhc->bqhc", rounded, valueset, preferred_element_type=jnp.float32
    ).astype(jnp.bfloat16)


def attend_backward(queries, keyset, valueset, grad_out):
    factor = HEAD_DIM ** (-0.5)
    scores = (
        jnp.einsum("bqhc,bkhc->bhqk", queries, keyset, preferred_element_type=jnp.float32) * factor
    )
    soft_weights = jax.nn.softmax(scores, axis=-1)
    rounded = soft_weights.astype(jnp.bfloat16)
    grad_value = jnp.einsum(
        "bhqk,bqhc->bkhc", rounded, grad_out, preferred_element_type=jnp.float32
    ).astype(jnp.bfloat16)
    grad_probs = jnp.einsum(
        "bqhc,bkhc->bhqk", grad_out, valueset, preferred_element_type=jnp.float32
    )
    delta_sum = jnp.sum(grad_probs * soft_weights, axis=-1, keepdims=True)
    grad_scores = (soft_weights * (grad_probs - delta_sum) * factor).astype(jnp.bfloat16)
    grad_query = jnp.einsum(
        "bhqk,bkhc->bqhc", grad_scores, keyset, preferred_element_type=jnp.float32
    ).astype(jnp.bfloat16)
    grad_key = jnp.einsum(
        "bhqk,bqhc->bkhc", grad_scores, queries, preferred_element_type=jnp.float32
    ).astype(jnp.bfloat16)
    return jnp.stack([grad_query, grad_key, grad_value], axis=2)


def heads_total(partial_rows):
    return lax.psum(partial_rows, "tensor")


def local(latents, noise, timesteps, ref_losses, weights):
    batch_count, row_count, model_width = (latents.shape[1], latents.shape[2], latents.shape[3])
    columns = weights.shape[3]
    heads_here = columns // HEAD_DIM
    frames_here = row_count // POSITIONS
    seq_count = lax.axis_size("seq")
    tokens_total = row_count * seq_count
    clean_rows = latents[0].astype(jnp.float32)
    target = noise[0].astype(jnp.float32)
    angle_value = (timesteps[0].astype(jnp.float32) / 1000.0 + 0.008) / 1.008 * (math.pi / 2)
    plan = (jnp.cos(angle_value) ** 2)[:, None, None]
    start_state = jnp.sqrt(plan) * clean_rows + jnp.sqrt(1.0 - plan) * target
    normed_one, inv_one = layer_norm(start_state)
    input_one = normed_one.astype(jnp.bfloat16)
    qkv_one = jnp.einsum(
        "btd,dje->btje", input_one, weights[:, 0, :3, :], preferred_element_type=jnp.float32
    ).astype(jnp.bfloat16)
    framed = qkv_one.reshape(batch_count * frames_here, POSITIONS, 3, heads_here, HEAD_DIM)
    attn_one = attend_forward(framed[:, :, 0], framed[:, :, 1], framed[:, :, 2]).reshape(
        batch_count, row_count, columns
    )
    state_one = start_state + heads_total(
        jnp.einsum("bte,de->btd", attn_one, weights[:, 0, 3, :], preferred_element_type=jnp.float32)
    )
    normed_two, inv_two = layer_norm(state_one)
    input_two = normed_two.astype(jnp.bfloat16)
    qkv_two = jnp.einsum(
        "btd,dje->btje", input_two, weights[:, 1, :3, :], preferred_element_type=jnp.float32
    ).astype(jnp.bfloat16)
    qkv_two = qkv_two.reshape(batch_count, frames_here, POSITIONS, 3, columns)
    piece = lax.all_to_all(qkv_two, "seq", split_axis=2, concat_axis=1, tiled=True)
    items = piece.shape[0]
    frames_all = piece.shape[1]
    piece_count = piece.shape[2]
    split_qkv = piece.reshape(items, frames_all, piece_count, 3, heads_here, HEAD_DIM).transpose(
        0, 2, 1, 3, 4, 5
    )
    split_qkv = split_qkv.reshape(items * piece_count, frames_all, 3, heads_here, HEAD_DIM)
    result = attend_forward(split_qkv[:, :, 0], split_qkv[:, :, 1], split_qkv[:, :, 2])
    result = result.reshape(items, piece_count, frames_all, columns).transpose(0, 2, 1, 3)
    attn_two = lax.all_to_all(result, "seq", split_axis=1, concat_axis=2, tiled=True).reshape(
        batch_count, row_count, columns
    )
    prediction = state_one + heads_total(
        jnp.einsum("bte,de->btd", attn_two, weights[:, 1, 3, :], preferred_element_type=jnp.float32)
    )
    diff_rows = prediction - target
    own_error = jnp.sum(diff_rows * diff_rows, axis=(1, 2))
    slot_mask = jnp.arange(2, dtype=jnp.int32) == lax.axis_index("pair")
    errors = lax.psum(jnp.where(slot_mask[:, None], own_error[None, :], 0.0), ("pair", "seq")) / (
        tokens_total * model_width
    )
    margin = errors[0] - ref_losses[0] - (errors[1] - ref_losses[1])
    dpo_loss = jnp.mean(jax.nn.softplus(beta_dpo * margin))
    signed = jnp.where(lax.axis_index("pair") == 0, 1.0, -1.0)
    coefficient = tokens_total * beta_dpo * jax.nn.sigmoid(beta_dpo * margin) * signed / batch_count
    grad_pred = coefficient[:, None, None] * 2.0 * diff_rows / model_width
    grad_two = grad_pred.astype(jnp.bfloat16)
    dout_two = jnp.einsum(
        "btd,de->bte", grad_two, weights[:, 1, 3, :], preferred_element_type=jnp.float32
    ).astype(jnp.bfloat16)
    dout_pos = lax.all_to_all(
        dout_two.reshape(batch_count, frames_here, POSITIONS, columns),
        "seq",
        split_axis=2,
        concat_axis=1,
        tiled=True,
    )
    frames_all, piece_count = (dout_pos.shape[1], dout_pos.shape[2])
    split_qkv = piece.reshape(
        batch_count, frames_all, piece_count, 3, heads_here, HEAD_DIM
    ).transpose(0, 2, 1, 3, 4, 5)
    split_qkv = split_qkv.reshape(batch_count * piece_count, frames_all, 3, heads_here, HEAD_DIM)
    split_grad = dout_pos.reshape(
        batch_count, frames_all, piece_count, heads_here, HEAD_DIM
    ).transpose(0, 2, 1, 3, 4)
    split_grad = split_grad.reshape(batch_count * piece_count, frames_all, heads_here, HEAD_DIM)
    dqkv_pos = attend_backward(
        split_qkv[:, :, 0], split_qkv[:, :, 1], split_qkv[:, :, 2], split_grad
    )
    dqkv_pos = dqkv_pos.reshape(batch_count, piece_count, frames_all, 3, columns).transpose(
        0, 2, 1, 3, 4
    )
    dqkv_two = lax.all_to_all(dqkv_pos, "seq", split_axis=1, concat_axis=2, tiled=True).reshape(
        batch_count, row_count, 3, columns
    )
    dnorm_two = heads_total(
        jnp.einsum(
            "btje,dje->btd", dqkv_two, weights[:, 1, :3, :], preferred_element_type=jnp.float32
        )
    )
    dstate = grad_pred + norm_backward(dnorm_two, normed_two, inv_two)
    grad_one = dstate.astype(jnp.bfloat16)
    dout_one = jnp.einsum(
        "btd,de->bte", grad_one, weights[:, 0, 3, :], preferred_element_type=jnp.float32
    ).astype(jnp.bfloat16)
    dout_framed = dout_one.reshape(batch_count * frames_here, POSITIONS, heads_here, HEAD_DIM)
    dqkv_one = attend_backward(
        framed[:, :, 0], framed[:, :, 1], framed[:, :, 2], dout_framed
    ).reshape(batch_count, row_count, 3, columns)
    flat_rows = batch_count * row_count
    input_one_flat = input_one.reshape(flat_rows, model_width)
    input_two_flat = input_two.reshape(flat_rows, model_width)
    grad_one_flat = grad_one.reshape(flat_rows, model_width)
    grad_two_flat = grad_two.reshape(flat_rows, model_width)
    dqkv_one_flat = dqkv_one.reshape(flat_rows, 3, columns)
    dqkv_two_flat = dqkv_two.reshape(flat_rows, 3, columns)
    attn_one_flat = attn_one.reshape(flat_rows, columns)
    attn_two_flat = attn_two.reshape(flat_rows, columns)
    first_block = jnp.concatenate(
        [
            jnp.einsum(
                "td,tje->dje", input_one_flat, dqkv_one_flat, preferred_element_type=jnp.float32
            ),
            jnp.einsum(
                "td,te->de", grad_one_flat, attn_one_flat, preferred_element_type=jnp.float32
            )[:, None],
        ],
        axis=1,
    )
    second_block = jnp.concatenate(
        [
            jnp.einsum(
                "td,tje->dje", input_two_flat, dqkv_two_flat, preferred_element_type=jnp.float32
            ),
            jnp.einsum(
                "td,te->de", grad_two_flat, attn_two_flat, preferred_element_type=jnp.float32
            )[:, None],
        ],
        axis=1,
    )
    grad_rows = lax.psum_scatter(
        jnp.stack([first_block, second_block], axis=1),
        ("pair", "seq"),
        scatter_dimension=0,
        tiled=True,
    )
    return (dpo_loss, grad_rows)


def solution(mesh):
    in_specs = (
        P("pair", None, "seq", None),
        P("pair", None, "seq", None),
        P("pair", None),
        P(),
        P(None, None, None, "tensor"),
    )
    out_specs = (P(), P(("pair", "seq"), None, None, "tensor"))
    return jax.shard_map(local, mesh=mesh, in_specs=in_specs, out_specs=out_specs, check_vma=False)
```

profile of v0, /device:TPU:1, one launch (start us, length us, event | category | flops | bytes accessed | tf_op | source)
XLA Modules:
  0.0 709.7 jit_solution(4275187458263335069)
XLA Ops:
  10.1 2.4 fusion.21
  14.8 2.7 convolution_bitcast_fusion.4
  17.6 54.4 %all-reduce.6.cloned.1.call-done = f32[1,256,1152]{2,1,0:T(8,128)} async-done(((f32[1,256,1152]{2,1,0:T(8,128)}), f32[1,256,1152]{2,1,0:T(8,128)}) %all-reduce.6.cloned.1.call-update) | async-done | bytes 1179664 | tf_op jit(solution)/shard_map/psum | solution.py:65
  73.9 3.2 fusion.31
  78.6 28.2 %all_to_all.16 = bf16[1,1,256,3,288]{4,3,1,0,2:T(4,128)(2,1)} all-to-all(bf16[1,1,256,3,288]{4,3,1,0,2:T(4,128)(2,1)S(1)} %copy.36), channel_id=1, replica_groups=mesh['pair'=2,'seq'=32,'tensor'=4] {'seq'}, dimensions={2} | all-to-all | bytes 884736 | tf_op jit(solution)/shard_map/all_to_all | solution.py:98
  106.7 2.6 reshape.512
  110.6 2.2 fusion.135
  113.8 17.5 %all_to_all.17 = bf16[1,32,8,288]{3,2,0,1:T(8,128)(2,1)S(1)} all-to-all(bf16[1,32,8,288]{3,2,0,1:T(8,128)(2,1)S(1)} %copy.41), channel_id=1, replica_groups=mesh['pair'=2,'seq'=32,'tensor'=4] {'seq'}, dimensions={1} | all-to-all | bytes 294912 | tf_op jit(solution)/shard_map/all_to_all | solution.py:108
  132.0 2.6 convolution_bitcast_fusion.3
  135.4 47.4 %all-reduce.8.cloned.1.call-done = f32[1,256,1152]{2,1,0:T(8,128)} async-done(((f32[1,256,1152]{2,1,0:T(8,128)}), f32[1,256,1152]{2,1,0:T(8,128)}) %all-reduce.8.cloned.1.call-update) | async-done | bytes 1179664 | tf_op jit(solution)/shard_map/psum | solution.py:65
  182.8 2.2 multiply_reduce_fusion.1
  186.1 131.4 %psum.30 = f32[2,1]{0,1:T(1,128)} all-reduce(f32[2,1]{0,1:T(1,128)} %compare_select_fusion), channel_id=1, replica_groups=mesh['pair'=2,'seq'=32,'tensor'=4] {'pair','seq'}, use_global_device_ids=true, to_apply=%region_11.12 | all-reduce | flops 2 | bytes 16 | tf_op jit(solution)/shard_map/psum | solution.py:117
  321.3 2.1 fusion.45
  323.5 1.9 copy.42
  325.9 3.3 reduce.15
  331.1 14.6 %all_to_all.18 = bf16[32,2,1152]{2,1,0:T(2,128)(2,1)} all-to-all(bf16[32,2,1152]{2,1,0:T(2,128)(2,1)} %reshape.515), channel_id=1, replica_groups=mesh['pair'=2,'seq'=32,'tensor'=4] {'seq'}, dimensions={0} | all-to-all | bytes 294912 | tf_op jit(solution)/shard_map/all_to_all | solution.py:129
  345.6 2.4 reshape.516
  348.0 2.8 bitcast_reduce_fusion
  352.6 2.1 fusion.96
  354.7 2.7 fusion.42
  357.4 2.6 fusion.43
  360.0 2.2 fusion.44
  364.1 1.9 stack.33
  374.6 19.0 %all_to_all.19 = bf16[1,32,8,3,288]{4,2,3,0,1:T(8,128)(2,1)S(1)} all-to-all(bf16[1,32,8,3,288]{4,2,3,0,1:T(8,128)(2,1)S(1)} %copy.48), channel_id=1, replica_groups=mesh['pair'=2,'seq'=32,'tensor'=4] {'seq'}, dimensions={1} | all-to-all | bytes 884736 | tf_op jit(solution)/shard_map/all_to_all | solution.py:151
  394.4 3.5 convolution_bitcast_fusion.2
  400.5 2.7 maximum_bitcast_fusion.1
  403.1 44.7 %all-reduce.10.cloned.1.call-done = f32[1,256,1152]{2,1,0:T(8,128)} async-done(((f32[1,256,1152]{2,1,0:T(8,128)}), f32[1,256,1152]{2,1,0:T(8,128)}) %all-reduce.10.cloned.1.call-update) | async-done | bytes 1179664 | tf_op jit(solution)/shard_map/psum | solution.py:65
  452.2 2.1 convolution_convert_fusion.6
  454.2 2.1 convolution_convert_fusion.5
  460.5 4.6 pad_maximum_fusion
  465.1 14.9 %copy.55 = f32[1152,2,4,288]{3,2,1,0:T(4,128)} copy(f32[1152,2,4,288]{0,3,2,1:T(8,128)} %pad_maximum_fusion) | data formatting | bytes 21233664 | tf_op jit(solution)/shard_map/stack | solution.py:200
  482.0 218.4 %all-reduce.12.cloned.1.call-done = f32[1152,2,4,288]{3,2,1,0:T(4,128)} async-done(((f32[1152,2,4,288]{3,2,1,0:T(4,128)}), f32[1152,2,4,288]{3,2,1,0:T(4,128)}) %all-reduce.12.cloned.1.call-update) | async-done | bytes 10616848
  (92 shorter events, 42.9 us)
Async XLA Ops:
  7.2 2.5 copy-start.1
  7.2 2.5 copy-start
  7.2 64.8 %all-reduce.6.cloned.1.call-start = ((), (), s32[]{:S(2)}) async-start(), calls=%async_computation.4 | async-start | bytes 2359296 | tf_op jit(solution)/shard_map/psum | solution.py:65
  12.5 2.3 copy-start.11
  14.1 0.7 copy-start.16
  14.8 2.7 copy-start.9
  17.6 165.2 %all-reduce.8.cloned.1.call-start = ((), (), s32[]{:S(2)}) async-start(), calls=%async_computation.5 | async-start | bytes 2359296 | tf_op jit(solution)/shard_map/psum | solution.py:65
  110.6 2.2 copy-start.8
  112.8 0.6 copy-start.15
  131.3 0.7 copy-start.7
  132.0 2.7 copy-start.13
  134.7 313.2 %all-reduce.10.cloned.1.call-start = ((), (), s32[]{:S(2)}) async-start(), calls=%async_computation.6 | async-start | bytes 2359296 | tf_op jit(solution)/shard_map/psum | solution.py:65
  393.6 0.8 copy-start.5
  397.9 302.5 %all-reduce.12.cloned.1.call-start = ((), (), s32[]{:S(2)}) async-start(), calls=%async_computation.7 | async-start | bytes 28311552
  398.2 1.4 copy-start.6
  447.9 1.7 copy-start.2
  450.1 2.1 copy-start.3
  450.1 1.7 copy-start.12
  450.1 2.1 copy-start.17
  456.3 1.1 copy-start.4
  456.4 1.1 copy-start.10
  457.8 2.2 slice-start
  458.7 1.8 slice-start.1
  480.0 0.7 copy-start.14
Sparse Core Ops, SparseCore 0:
  17.7 54.2 all-reduce.5
  134.8 47.9 all-reduce.7
  398.0 49.7 all-reduce.9
  480.1 220.2 all-reduce.11
where the time goes:
time: 712 us; the launch traced here: 710 us
  waiting for transfers between devices  365 us (51%)
  blocking collectives  211 us (30%)
  local copies, waits for them, and re-layouts  50.4 us (7%)
  matrix products  41.6 us (6%)
  other arithmetic  22.1 us (3%)
  between operations  19.5 us (3%)
    unnamed x5, waiting for transfers between devices  218 us
    psum x3, waiting for transfers between devices, heads_total(): return lax.psum(partial_rows, 'tensor')  146 us
    psum x1, blocking collectives, local(): lax.psum(jnp.where(slot_mask[:, None], own_error[None, :], 0.0), ('pair',...  131 us
    all_to_all x1, blocking collectives, local(): lax.all_to_all(qkv_two, 'seq', split_axis=2, concat_axis=1, tiled=True)  28.2 us
    all_to_all x1, blocking collectives, local(): lax.all_to_all(dqkv_pos, 'seq', split_axis=1, concat_axis=2, tiled=True)  19 us
    all_to_all x1, blocking collectives, local(): lax.all_to_all(result, 'seq', split_axis=1, concat_axis=2, tiled=True)  17.5 us
    another operation x1, local copies, waits for them, and re-layouts, local(): jnp.stack([first_block, second_block], axis=1)  14.9 us
    all_to_all x1, blocking collectives, local(): lax.all_to_all(dout_two.reshape(batch_count, frames_here, POSITIONS, colu...  14.6 us
  transfers between devices with their start and end apart: 4, of which 4 were waited for; matrix products, arithmetic and copies ran while one was open for 1% of the time, Pallas kernels for 0%

commit v1 on v0

v1 whole, which is shorter than its diff:
```python
import functools
import math

import jax
import jax.numpy as jnp
from jax import lax
from jax.experimental import pallas as pl
from jax.experimental.pallas import tpu as pltpu
from jax.sharding import PartitionSpec as P

HEAD_DIM = 72
LANES = 384
NY = 4
MESH = pl.DeviceIdType.MESH
BF = jnp.bfloat16
F32 = jnp.float32

beta_dpo = 0.5
norm_eps = 1e-06


def dot(a, b):
    return jnp.dot(a, b, preferred_element_type=F32)


def dot_nt(a, b):
    return lax.dot_general(a, b, (((1,), (1,)), ((), ())), preferred_element_type=F32)


def dot_tn(a, b):
    return lax.dot_general(a, b, (((0,), (0,)), ((), ())), preferred_element_type=F32)


def iota(shape, axis):
    return lax.broadcasted_iota(jnp.int32, shape, axis)


def head_mask(head, dtype):
    lane = iota((1, LANES), 1)
    return ((lane >= head * HEAD_DIM) & (lane < (head + 1) * HEAD_DIM)).astype(dtype)


def attend_forward(heads, qkv_ref, probs_ref, out_ref, mask):
    queries = qkv_ref[:, :LANES]
    keys = qkv_ref[:, LANES : 2 * LANES]
    values = qkv_ref[:, 2 * LANES :]
    total = None
    for head in range(heads):
        scores = dot_nt(queries * head_mask(head, BF), keys) * (HEAD_DIM**-0.5)
        if mask is not None:
            scores = jnp.where(mask, scores, -1e30)
        scores = jnp.exp(scores - jnp.max(scores, axis=1, keepdims=True))
        probs = scores * (1.0 / jnp.sum(scores, axis=1, keepdims=True))
        probs_ref[head] = probs
        part = dot(probs.astype(BF), values) * head_mask(head, F32)
        total = part if total is None else total + part
    out_ref[...] = total.astype(BF)


def attend_backward(heads, qkv_ref, probs_ref, grad_ref, dqkv_ref):
    queries = qkv_ref[:, :LANES]
    keys = qkv_ref[:, LANES : 2 * LANES]
    values = qkv_ref[:, 2 * LANES :]
    grad = grad_ref[...]
    sums = [None, None, None]
    for head in range(heads):
        probs = probs_ref[head]
        dprobs = dot_nt(grad * head_mask(head, BF), values)
        delta = jnp.sum(dprobs * probs, axis=1, keepdims=True)
        dscores = (probs * (dprobs - delta) * (HEAD_DIM**-0.5)).astype(BF)
        parts = (dot(dscores, keys), dot_tn(dscores, queries), dot_tn(probs.astype(BF), grad))
        for slot in range(3):
            part = parts[slot] * head_mask(head, F32)
            sums[slot] = part if sums[slot] is None else sums[slot] + part
    for slot in range(3):
        dqkv_ref[:, slot * LANES : (slot + 1) * LANES] = sums[slot].astype(BF)


def compact(dqkv_ref):
    dq = dqkv_ref[:, :LANES].astype(F32)
    dk = pltpu.roll(dqkv_ref[:, LANES : 2 * LANES].astype(F32), 32, 1)
    dv = pltpu.roll(dqkv_ref[:, 2 * LANES :].astype(F32), 64, 1)
    return jnp.concatenate(
        [
            dq[:, :256],
            dq[:, 256:] + dk[:, :128],
            dk[:, 128:256],
            dk[:, 256:] + dv[:, :128],
            dv[:, 128:],
        ],
        axis=1,
    ).astype(BF)


def weight_grads(input_ref, compact_ref, grad_ref, attn_ref, out_ref, half_rows):
    attn = pltpu.roll(attn_ref[...].astype(F32), 96, 1).astype(BF)
    dqkv = compact_ref[...]
    step = 128
    for start in range(0, 2 * half_rows, step):
        first = dot_tn(input_ref[:, start : start + step], dqkv)
        second = dot_tn(grad_ref[:, start : start + step], attn)
        rows = jnp.concatenate(
            [first[:, :768], first[:, 768:] + second[:, :128], second[:, 128:]], axis=1
        ).astype(BF)
        done = 0
        while done < step:
            half, at = divmod(start + done, half_rows)
            size = min(step - done, half_rows - at)
            out_ref[half, at : at + size, :] = rows[done : done + size]
            done += size


def pack_matrix(peers, tokens):
    shape = (8 * peers, 3 * peers * tokens)
    row, col = iota(shape, 0), iota(shape, 1)
    peer, inner = row // 8, row % 8
    source = (inner // tokens) * (peers * tokens) + peer * tokens + inner % tokens
    return ((inner < 3 * tokens) & (col == source)).astype(F32).astype(BF)


def unpack_matrix(peers, tokens, third):
    shape = (peers * tokens, 8 * peers)
    token, col = iota(shape, 0), iota(shape, 1)
    source = (token // tokens) * 8 + third * tokens + token % tokens
    return (col == source).astype(F32).astype(BF)


def pack(rows, matrix, peers):
    third = rows.shape[1] // 3
    stacked = jnp.concatenate(
        [rows[:, :third], rows[:, third : 2 * third], rows[:, 2 * third :]], axis=0
    )
    return dot(matrix, stacked).reshape(peers, 8, third)


def unpack(messages, matrices, peers):
    flat = messages.reshape(8 * peers, messages.shape[2]).astype(BF)
    return jnp.concatenate([dot(matrix, flat) for matrix in matrices], axis=1)


def remote(src, dst, send, recv, device):
    return pltpu.make_async_remote_copy(
        src_ref=src,
        dst_ref=dst,
        send_sem=send,
        recv_sem=recv,
        device_id=device,
        device_id_type=MESH,
    )


class RingSum:
    def __init__(self, blocks, low, high, send, recv, me, device, cut):
        self.blocks, self.low, self.high, self.me, self.cut = blocks, low, high, me, cut
        self.right, self.left = (me + 1) % 4, (me + 3) % 4
        opposite = (me + 2) % 4
        rows = blocks.shape[1]
        self.lo, self.hi = pl.ds(0, cut), pl.ds(cut, rows - cut)
        right, left = device(self.right), device(self.left)

        def copy(block, half, dst, index, to):
            return remote(blocks.at[block, half], dst, send.at[index], recv.at[index], to)

        self.far_right = copy(opposite, self.lo, low.at[0], 0, right)
        self.far_left = copy(opposite, self.hi, high.at[0], 1, left)
        self.near_right = copy(self.right, self.hi, high.at[2], 2, right)
        self.near_left = copy(self.left, self.lo, low.at[2], 3, left)
        self.sum_right = copy(self.right, self.lo, low.at[1], 4, right)
        self.sum_left = copy(self.left, self.hi, high.at[1], 5, left)

    def start(self):
        self.far_right.start()
        self.far_left.start()
        self.near_right.start()
        self.near_left.start()

    def middle(self):
        self.far_right.wait_recv()
        own = self.blocks[self.right, self.lo].astype(F32)
        self.blocks[self.right, self.lo] = (own + self.low[0].astype(F32)).astype(BF)
        self.sum_right.start()
        self.far_left.wait_recv()
        own = self.blocks[self.left, self.hi].astype(F32)
        self.blocks[self.left, self.hi] = (own + self.high[0].astype(F32)).astype(BF)
        self.sum_left.start()

    def finish(self):
        self.near_right.wait_recv()
        self.near_left.wait_recv()
        self.sum_right.wait_recv()
        self.sum_left.wait_recv()
        for copy in (self.far_right, self.far_left, self.near_right, self.near_left):
            copy.wait_send()
        self.sum_right.wait_send()
        self.sum_left.wait_send()
        low = self.blocks[self.me, self.lo].astype(F32)
        high = self.blocks[self.me, self.hi].astype(F32)
        low = low + self.low[1].astype(F32) + self.low[2].astype(F32)
        high = high + self.high[1].astype(F32) + self.high[2].astype(F32)
        return jnp.concatenate([low, high], axis=0)


class RingGather:
    def __init__(self, blocks, send, recv, me, device):
        self.right, self.left = (me + 1) % 4, (me + 3) % 4
        half = blocks.shape[1] // 2
        lo, hi = pl.ds(0, half), pl.ds(half, half)
        right, left = device(self.right), device(self.left)

        def copy(block, part, index, to):
            ref = blocks.at[block, part]
            return remote(ref, ref, send.at[index], recv.at[index], to)

        self.first_right = copy(me, lo, 0, right)
        self.first_left = copy(me, hi, 1, left)
        self.next_right = copy(me, hi, 2, right)
        self.next_left = copy(me, lo, 3, left)
        self.pass_right = copy(self.left, lo, 4, right)
        self.pass_left = copy(self.right, hi, 5, left)

    def start(self):
        self.first_right.start()
        self.first_left.start()
        self.next_right.start()
        self.next_left.start()

    def middle(self):
        self.first_right.wait_recv()
        self.pass_right.start()
        self.first_left.wait_recv()
        self.pass_left.start()

    def finish(self):
        for copy in (self.next_right, self.next_left, self.pass_right, self.pass_left):
            copy.wait_recv()
        for copy in (
            self.first_right,
            self.first_left,
            self.next_right,
            self.next_left,
            self.pass_right,
            self.pass_left,
        ):
            copy.wait_send()


class Exchange:
    def __init__(self, out, into, send, recv, me, peers, device):
        self.out, self.into, self.send, self.recv = out, into, send, recv
        self.me, self.peers, self.device = me, peers, device

    def start(self):
        def step(offset, carry):
            peer = (self.me + offset) % self.peers
            remote(
                self.out.at[peer], self.into.at[self.me], self.send, self.recv, self.device(peer)
            ).start()
            return carry

        lax.fori_loop(1, self.peers, step, 0)
        self.into[self.me] = self.out[self.me]

    def finish(self):
        every = pl.ds(0, self.peers - 1)
        remote(
            self.out.at[every],
            self.into.at[every],
            self.send,
            self.recv,
            self.device((self.me + 1) % self.peers),
        ).wait()


def kernel(
    peers,
    heads,
    scale_ref,
    latent_ref,
    noise_ref,
    weights_hbm,
    grads_out,
    errors_out,
    weights_ref,
    weights_sem,
    input_one,
    qkv_one,
    qkv_two,
    probs_one,
    probs_two,
    attn_one,
    attn_two,
    dout_ref,
    dqkv_ref,
    compact_ref,
    start_pos,
    noise_pos,
    state_ref,
    norm_ref,
    grad_ref,
    sum_blocks,
    sum_low,
    sum_high,
    sum_send,
    sum_recv,
    gather_blocks,
    gather_send,
    gather_recv,
    first_out,
    first_in,
    swap_out,
    swap_in,
    swap_send,
    swap_recv,
    partial_ref,
    pair_in,
    pair_send,
    pair_recv,
    y_blocks,
    y_low,
    y_high,
    y_send,
    y_recv,
    z_out,
    z_in,
    z_send,
    z_recv,
    err_x,
    err_x_send,
    err_x_recv,
    err_pair,
    err_pair_send,
    err_pair_recv,
):
    pair, seq, x = lax.axis_index("pair"), lax.axis_index("seq"), lax.axis_index("tensor")
    planes = peers // NY
    y, z = seq // planes, seq % planes
    rows, width = latent_ref.shape
    quarter = rows // 4
    tokens = quarter // peers
    half_rows = width // 2
    y_rows = half_rows // NY
    out_rows = y_rows // planes
    z_rows = z_out.shape[2]

    def at_x(index):
        return (pair, seq, index)

    def at_y(index):
        return (pair, index * planes + z, x)

    def at_z(index):
        return (pair, y * planes + index, x)

    def at_seq(index):
        return (pair, index, x)

    other = (1 - pair, seq, x)

    loads = [
        pltpu.make_async_copy(weights_hbm.at[block], weights_ref.at[block], weights_sem.at[block])
        for block in range(2)
    ]
    for load in loads:
        load.start()

    barrier = pltpu.get_barrier_semaphore()

    def greet(offset, carry):
        pl.semaphore_signal(
            barrier, inc=1, device_id=at_seq((seq + offset) % peers), device_id_type=MESH
        )
        return carry

    lax.fori_loop(1, peers, greet, 0)
    for offset in range(1, 4):
        pl.semaphore_signal(
            barrier, inc=1, device_id=at_x((x + offset) % 4), device_id_type=MESH
        )
    pl.semaphore_signal(barrier, inc=1, device_id=other, device_id_type=MESH)

    ring_sums = [
        RingSum(
            sum_blocks.at[use],
            sum_low.at[use],
            sum_high.at[use],
            sum_send.at[use],
            sum_recv.at[use],
            x,
            at_x,
            quarter // 2,
        )
        for use in range(3)
    ]
    gathers = [
        RingGather(gather_blocks.at[use], gather_send.at[use], gather_recv.at[use], x, at_x)
        for use in range(3)
    ]
    first = Exchange(first_out, first_in, swap_send.at[0], swap_recv.at[0], seq, peers, at_seq)
    swaps = [
        Exchange(
            swap_out.at[use],
            swap_in.at[use],
            swap_send.at[use + 1],
            swap_recv.at[use + 1],
            seq,
            peers,
            at_seq,
        )
        for use in range(2)
    ]
    y_sums = [
        RingSum(
            y_blocks.at[use],
            y_low.at[use],
            y_high.at[use],
            y_send.at[use],
            y_recv.at[use],
            y,
            at_y,
            y_low.shape[2],
        )
        for use in range(2)
    ]
    z_swaps = [
        Exchange(z_out.at[use], z_in.at[use], z_send.at[use], z_recv.at[use], z, planes, at_z)
        for use in range(2)
    ]
    pairs = [
        remote(
            partial_ref.at[use, 1 - pair],
            pair_in.at[use],
            pair_send.at[use],
            pair_recv.at[use],
            other,
        )
        for use in range(2)
    ]

    packing = pack_matrix(peers, tokens)
    unpacking = [unpack_matrix(peers, tokens, third) for third in range(3)]
    clean_scale, noise_scale = scale_ref[0], scale_ref[1]

    mine = pl.ds(pl.multiple_of(x * quarter, quarter), quarter)
    first_out[...] = jnp.concatenate(
        [
            pack(latent_ref[mine, :], packing, peers),
            pack(noise_ref[mine, :], packing, peers),
        ],
        axis=1,
    ).astype(BF)
    pl.semaphore_wait(barrier, peers + 3)
    first.start()

    state = clean_scale * latent_ref[...].astype(F32) + noise_scale * noise_ref[...].astype(F32)
    center = state - jnp.mean(state, axis=1, keepdims=True)
    inv_std = lax.rsqrt(jnp.mean(center * center, axis=1, keepdims=True) + norm_eps)
    input_one[...] = (center * inv_std).astype(BF)
    loads[0].wait()
    qkv_one[...] = dot(input_one[...], weights_ref[0, :, : 3 * LANES]).astype(BF)
    attend_forward(heads, qkv_one, probs_one, attn_one, None)
    sum_blocks[0] = (
        dot_nt(attn_one[...], weights_ref[0, :, 3 * LANES :]).reshape(4, quarter, width).astype(BF)
    )
    ring_sums[0].start()
    ring_sums[0].middle()
    out_one = ring_sums[0].finish()

    swap_out[0] = pack(out_one.astype(BF), packing, peers).astype(BF)
    swaps[0].start()
    first.finish()
    messages = first_in[...].astype(F32)
    clean = unpack(messages[:, :8], unpacking, peers)
    noise_pos[...] = unpack(messages[:, 8:], unpacking, peers)
    start_pos[...] = clean_scale * clean + noise_scale * noise_pos[...]
    swaps[0].finish()
    state = start_pos[...] + unpack(swap_in[0].astype(F32), unpacking, peers)
    state_ref[...] = state
    center = state - jnp.mean(state, axis=1, keepdims=True)
    inv_two = lax.rsqrt(jnp.mean(center * center, axis=1, keepdims=True) + norm_eps)
    norm_ref[...] = center * inv_two
    gather_blocks[0, x] = norm_ref[...].astype(BF)
    gathers[0].start()
    gathers[0].middle()
    gathers[0].finish()

    input_two = gather_blocks.at[0]
    loads[1].wait()
    row, col = iota((rows, rows), 0), iota((rows, rows), 1)
    same = (row // quarter == col // quarter) & (row % tokens == col % tokens)
    flat = input_two[...].reshape(rows, width)
    qkv_two[...] = dot(flat, weights_ref[1, :, : 3 * LANES]).astype(BF)
    attend_forward(heads, qkv_two, probs_two, attn_two, same)
    sum_blocks[1] = (
        dot_nt(attn_two[...], weights_ref[1, :, 3 * LANES :]).reshape(4, quarter, width).astype(BF)
    )
    ring_sums[1].start()
    ring_sums[1].middle()
    diff = state_ref[...] + ring_sums[1].finish() - noise_pos[...]
    error = jnp.sum(jnp.sum(diff * diff, axis=1, keepdims=True), axis=0, keepdims=True)
    sign = 1.0 - 2.0 * pair.astype(F32)
    grad = diff * (2.0 * sign / width)
    grad_ref[...] = grad
    gather_blocks[1, x] = grad.astype(BF)
    gathers[1].start()
    gathers[1].middle()
    gathers[1].finish()

    flat = gather_blocks[1].reshape(rows, width)
    dout_ref[...] = dot(flat, weights_ref[1, :, 3 * LANES :]).astype(BF)
    attend_backward(heads, qkv_two, probs_two, dout_ref, dqkv_ref)
    sum_blocks[2] = (
        dot_nt(dqkv_ref[...], weights_ref[1, :, : 3 * LANES])
        .reshape(4, quarter, width)
        .astype(BF)
    )
    ring_sums[2].start()
    compact_ref[...] = compact(dqkv_ref)
    ring_sums[2].middle()

    def flat_view(use):
        return lambda start, size: gather_blocks[use, :, :, start : start + size].reshape(
            rows, size
        )

    class View:
        def __init__(self, use):
            self.read = flat_view(use)

        def __getitem__(self, index):
            lanes = index[1]
            return self.read(lanes.start, lanes.stop - lanes.start)

    weight_grads(View(0), compact_ref, View(1), attn_two, partial_ref.at[0], half_rows)
    pairs[0].start()
    dnorm = ring_sums[2].finish()
    normed = norm_ref[...]
    mean_grad = jnp.mean(dnorm, axis=1, keepdims=True)
    mean_prod = jnp.mean(dnorm * normed, axis=1, keepdims=True)
    dstate = grad_ref[...] + inv_two * (dnorm - mean_grad - normed * mean_prod)

    messages = pack(dstate.astype(BF), packing, peers)
    inner = iota(messages.shape, 1)
    error_high = error.astype(BF).astype(F32)
    error_low = error - error_high
    messages = jnp.where(inner == 6, error_high.reshape(1, 1, 1), messages)
    messages = jnp.where(inner == 7, error_low.reshape(1, 1, 1), messages)
    swap_out[1] = messages.astype(BF)
    swaps[1].start()

    def reduce_pair(use):
        pairs[use].wait()
        own = partial_ref[use, pair].astype(F32) + pair_in[use].astype(F32)
        y_blocks[use] = own.astype(BF).reshape(NY, y_rows, width)

    shape = (planes * z_rows, y_rows)
    row, col = iota(shape, 0), iota(shape, 1)
    spread = (row % z_rows < out_rows) & (col == (row // z_rows) * out_rows + row % z_rows)
    spread = spread.astype(F32).astype(BF)

    def start_z(use):
        rows_here = y_sums[use].finish().astype(BF)
        z_out[use] = dot(spread, rows_here).reshape(planes, z_rows, width).astype(BF)
        z_swaps[use].start()

    def finish_z(use):
        z_swaps[use].finish()
        grads_out[1 - use] = jnp.sum(z_in[use].astype(F32), axis=0)

    reduce_pair(0)
    y_sums[0].start()
    swaps[1].finish()
    messages = swap_in[1].astype(F32)
    gather_blocks[2, x] = unpack(messages, unpacking, peers).astype(BF)
    gathers[2].start()
    total = jnp.sum(messages, axis=0)
    err_x[x] = jnp.broadcast_to(total[6:7, :128] + total[7:8, :128], (8, 128))
    err_copies = [
        remote(
            err_x.at[x],
            err_x.at[x],
            err_x_send.at[offset - 1],
            err_x_recv.at[offset - 1],
            at_x((x + offset) % 4),
        )
        for offset in range(1, 4)
    ]
    for copy in err_copies:
        copy.start()
    gathers[2].middle()
    y_sums[0].middle()
    gathers[2].finish()

    flat = gather_blocks[2].reshape(rows, width)
    dout_ref[...] = dot(flat, weights_ref[0, :, 3 * LANES :]).astype(BF)
    start_z(0)
    for copy in err_copies:
        copy.wait()
    err_pair[pair] = jnp.sum(err_x[...], axis=0)
    err_copy = remote(
        err_pair.at[pair], err_pair.at[pair], err_pair_send, err_pair_recv, other
    )
    err_copy.start()
    attend_backward(heads, qkv_one, probs_one, dout_ref, dqkv_ref)
    compact_ref[...] = compact(dqkv_ref)
    weight_grads(input_one, compact_ref, View(2), attn_one, partial_ref.at[1], half_rows)
    pairs[1].start()
    finish_z(0)
    err_copy.wait()
    errors_out[...] = err_pair[...]
    reduce_pair(1)
    y_sums[1].start()
    y_sums[1].middle()
    start_z(1)
    finish_z(1)


def local(latents, noise, timesteps, ref_losses, weights):
    width, columns = weights.shape[0], weights.shape[3]
    rows = latents.shape[2]
    peers = lax.axis_size("seq")
    quarter = rows // 4
    planes = peers // NY
    half_rows = width // 2
    y_rows = half_rows // NY
    y_cut = (y_rows // 32 + 1) * 16
    out_rows = y_rows // planes
    z_rows = -(-out_rows // 8) * 8
    heads = columns // HEAD_DIM
    tokens_total = rows * peers

    angle = (timesteps[0, 0].astype(F32) / 1000.0 + 0.008) / 1.008 * (math.pi / 2)
    plan = jnp.cos(angle) ** 2
    scales = jnp.stack([jnp.sqrt(plan), jnp.sqrt(1.0 - plan)])
    padded = jnp.pad(weights, ((0, 0), (0, 0), (0, 0), (0, LANES - columns)))
    padded = padded.transpose(1, 0, 2, 3).reshape(2, width, 4 * LANES)

    vmem = pltpu.VMEM
    dma = pltpu.SemaphoreType.DMA
    third = width // 3
    grads, errors = pl.pallas_call(
        functools.partial(kernel, peers, heads),
        out_shape=(
            jax.ShapeDtypeStruct((2, z_rows, width), F32),
            jax.ShapeDtypeStruct((2, 8, 128), F32),
        ),
        in_specs=[
            pl.BlockSpec(memory_space=pltpu.SMEM),
            pl.BlockSpec(memory_space=vmem),
            pl.BlockSpec(memory_space=vmem),
            pl.BlockSpec(memory_space=pl.ANY),
        ],
        out_specs=(pl.BlockSpec(memory_space=vmem), pl.BlockSpec(memory_space=vmem)),
        scratch_shapes=[
            vmem((2, width, 4 * LANES), BF),
            dma((2,)),
            vmem((rows, width), BF),
            vmem((rows, 3 * LANES), BF),
            vmem((rows, 3 * LANES), BF),
            vmem((heads, rows, rows), F32),
            vmem((heads, rows, rows), F32),
            vmem((rows, LANES), BF),
            vmem((rows, LANES), BF),
            vmem((rows, LANES), BF),
            vmem((rows, 3 * LANES), BF),
            vmem((rows, 896), BF),
            vmem((quarter, width), F32),
            vmem((quarter, width), F32),
            vmem((quarter, width), F32),
            vmem((quarter, width), F32),
            vmem((quarter, width), F32),
            vmem((3, 4, quarter, width), BF),
            vmem((3, 3, quarter // 2, width), BF),
            vmem((3, 3, quarter // 2, width), BF),
            dma((3, 6)),
            dma((3, 6)),
            vmem((3, 4, quarter, width), BF),
            dma((3, 6)),
            dma((3, 6)),
            vmem((peers, 16, third), BF),
            vmem((peers, 16, third), BF),
            vmem((2, peers, 8, third), BF),
            vmem((2, peers, 8, third), BF),
            dma((3,)),
            dma((3,)),
            vmem((2, 2, half_rows, width), BF),
            vmem((2, half_rows, width), BF),
            dma((2,)),
            dma((2,)),
            vmem((2, NY, y_rows, width), BF),
            vmem((2, 3, y_cut, width), BF),
            vmem((2, 3, y_rows - y_cut, width), BF),
            dma((2, 6)),
            dma((2, 6)),
            vmem((2, planes, z_rows, width), BF),
            vmem((2, planes, z_rows, width), BF),
            dma((2,)),
            dma((2,)),
            vmem((4, 8, 128), F32),
            dma((3,)),
            dma((3,)),
            vmem((2, 8, 128), F32),
            dma,
            dma,
        ],
        compiler_params=pltpu.CompilerParams(
            collective_id=0, has_side_effects=True, vmem_limit_bytes=60 * 2**20
        ),
    )(scales, latents[0, 0], noise[0, 0], padded)

    errors = errors[:, 0, 0] / (tokens_total * width)
    margin = errors[0] - ref_losses[0, 0] - (errors[1] - ref_losses[1, 0])
    dpo_loss = jax.nn.softplus(beta_dpo * margin)
    coefficient = tokens_total * beta_dpo * jax.nn.sigmoid(beta_dpo * margin)
    grads = grads[:, :out_rows].reshape(2, out_rows, 4, columns).transpose(1, 0, 2, 3)
    return (dpo_loss, grads * coefficient)


def solution(mesh):
    in_specs = (
        P("pair", None, "seq", None),
        P("pair", None, "seq", None),
        P("pair", None),
        P(),
        P(None, None, None, "tensor"),
    )
    out_specs = (P(), P(("pair", "seq"), None, None, "tensor"))
    return jax.shard_map(local, mesh=mesh, in_specs=in_specs, out_specs=out_specs, check_vma=False)
```

time: 712 us -> 146 us (0.21)
  waiting for transfers between devices: 365 us -> 0 us
  blocking collectives: 211 us -> 0 us
  Pallas kernels: 0 us -> 119 us
  matrix products: 41.6 us -> 0 us
  local copies, waits for them, and re-layouts: 50.4 us -> 18.8 us
  other arithmetic: 22.1 us -> 2.26 us
  between operations: 19.5 us -> 5.3 us
    unnamed x5 -> x0, waiting for transfers between devices: 218 us -> none
    psum x3 -> x0, waiting for transfers between devices: 146 us -> none  [heads_total(): return lax.psum(partial_rows, 'tensor')]
    psum x1 -> x0, blocking collectives: 131 us -> none  [local(): lax.psum(jnp.where(slot_mask[:, None], own_error[None, :], 0.0), ('pair',...]
    pallas_call x0 -> x1, Pallas kernels: none -> 119 us  [local(): pl.pallas_call(functools.partial(kernel, peers, heads), out_shape=(jax.Sh...]
    all_to_all x4 -> x0, blocking collectives: 79.3 us -> none  [the longest x1 28.2 us: local(): lax.all_to_all(qkv_two, 'seq', split_axis=2, concat_axis=1, tiled=True)]
    dot_general x21 -> x0, matrix products: 37.9 us -> none  [the longest x2 4.79 us: attend_backward(): jnp.einsum('bhqk,bkhc->bqhc', grad_scores, keyset, preferred_element_type...]
    another operation x4 -> x0, local copies, waits for them, and re-layouts: 20.5 us -> none  [the longest x1 14.9 us: local(): jnp.stack([first_block, second_block], axis=1)]
    unnamed x45 -> x2, local copies, waits for them, and re-layouts: 11 us -> 0.01 us
  transfers between devices with their start and end apart: 4 -> 0, of which waited for: 4 -> 0; matrix products, arithmetic and copies ran while one was open for 1% -> 0% of each run, Pallas kernels for 0% -> 0%
where the time goes in v1:
time: 146 us; the launch traced here: 145 us
  Pallas kernels  119 us (82%)
  local copies, waits for them, and re-layouts  18.8 us (13%)
  between operations  5.3 us (4%)
  other arithmetic  2.26 us (2%)
    pallas_call x1, Pallas kernels, local(): pl.pallas_call(functools.partial(kernel, peers, heads), out_shape=(jax.Sh...  119 us
    reshape x1, local copies, waits for them, and re-layouts, local(): padded = padded.transpose(1, 0, 2, 3).reshape(2, width, 4 * LANES)  10.3 us
    pad x1, local copies, waits for them, and re-layouts, local(): padded = jnp.pad(weights, ((0, 0), (0, 0), (0, 0), (0, LANES - columns)))  6.38 us

profile of v1, /device:TPU:1, one launch (start us, length us, event | category | flops | bytes accessed | tf_op | source)
XLA Modules:
  0.0 145.3 jit_solution(3065408232263987984)
XLA Ops:
  1.4 0.6 pad_maximum_fusion.scale_ref
  2.1 6.4 %pad.4 = bf16[1152,2,4,384]{0,3,2,1:T(8,128)(2,1)} pad(bf16[1152,2,4,288]{0,3,2,1:T(8,128)(2,1)} %param.9, bf16[]{:T(256)} %constant.23.clone.1), padding=0_0x0_0x0_0x0_96 | pad | bytes 12386306 | tf_op jit(solution)/shard_map/jit(_pad)/pad | solution.py:634
  8.4 10.3 %copy.11.weights_hbm = bf16[2,1152,1536]{2,1,0:T(8,128)(2,1)} copy(bf16[2,1152,1536]{1,2,0:T(8,128)(2,1)} %bitcast.14) | data formatting | bytes 14155776 | tf_op jit(solution)/shard_map/reshape | solution.py:635
  18.7 0.0 copy-start
  18.7 118.9 %shard_map.68 = (f32[2,24,1152]{2,1,0:T(8,128)}, f32[2,8,128]{2,1,0:T(8,128)}) custom-call(f32[2]{0:T(128)} %pad_maximum_fusion.scale_ref, bf16[256,1152]{1,0:T(8,128)(2,1)} %bitcast.15, bf16[256,1152]{1,0:T(8,128)(2,1)} %bitcast.16, bf16[2,1152,1536]{2,1,0:T(8,128)(2,1)} %copy.11.weights_hbm), custom_call_target="tpu_custom_call" | custom-call | tf_op jit(solution)/shard_map/pallas_call | solution.py:640
  137.6 0.7 slice_multiply_fusion.1
  138.3 0.5 fusion
  138.9 0.0 copy-done
  138.9 0.6 fusion.1
  142.2 1.0 slice_multiply_fusion
  143.1 0.1 copy.10
  143.2 1.0 mul.27
Async XLA Ops:
  18.7 120.2 %copy-start = (f32[2,1]{0,1:T(1,128)S(1)}, f32[2,1]{0,1:T(1,128)}, u32[]{:S(2)}) copy-start(f32[2,1]{0,1:T(1,128)} %param.8) | copy-start | bytes 28

commit v2 on v1

--- a/solution.py
+++ b/solution.py
@@ -275,11 +275,12 @@
     peers,
     heads,
     scale_ref,
+    ref_losses,
     latent_ref,
     noise_ref,
     weights_hbm,
     grads_out,
-    errors_out,
+    loss_out,
     weights_ref,
     weights_sem,
     input_one,
@@ -356,12 +357,25 @@
 
     other = (1 - pair, seq, x)
 
+    columns = weights_hbm.shape[2]
     loads = [
-        pltpu.make_async_copy(weights_hbm.at[block], weights_ref.at[block], weights_sem.at[block])
+        [
+            pltpu.make_async_copy(
+                weights_hbm.at[block, slot],
+                weights_ref.at[block, pl.ds(slot * LANES, columns)],
+                weights_sem.at[block, slot],
+            )
+            for slot in range(4)
+        ]
         for block in range(2)
     ]
-    for load in loads:
+    for load in loads[0] + loads[1]:
         load.start()
+    for slot in range(4):
+        for block in range(2):
+            weights_ref[block, slot * LANES + columns : (slot + 1) * LANES, :] = jnp.zeros(
+                (LANES - columns, width), BF
+            )
 
     barrier = pltpu.get_barrier_semaphore()
 
@@ -455,11 +469,12 @@
     center = state - jnp.mean(state, axis=1, keepdims=True)
     inv_std = lax.rsqrt(jnp.mean(center * center, axis=1, keepdims=True) + norm_eps)
     input_one[...] = (center * inv_std).astype(BF)
-    loads[0].wait()
-    qkv_one[...] = dot(input_one[...], weights_ref[0, :, : 3 * LANES]).astype(BF)
+    for load in loads[0]:
+        load.wait()
+    qkv_one[...] = dot_nt(input_one[...], weights_ref[0, : 3 * LANES]).astype(BF)
     attend_forward(heads, qkv_one, probs_one, attn_one, None)
     sum_blocks[0] = (
-        dot_nt(attn_one[...], weights_ref[0, :, 3 * LANES :]).reshape(4, quarter, width).astype(BF)
+        dot(attn_one[...], weights_ref[0, 3 * LANES :]).reshape(4, quarter, width).astype(BF)
     )
     ring_sums[0].start()
     ring_sums[0].middle()
@@ -484,14 +499,15 @@
     gathers[0].finish()
 
     input_two = gather_blocks.at[0]
-    loads[1].wait()
+    for load in loads[1]:
+        load.wait()
     row, col = iota((rows, rows), 0), iota((rows, rows), 1)
     same = (row // quarter == col // quarter) & (row % tokens == col % tokens)
     flat = input_two[...].reshape(rows, width)
-    qkv_two[...] = dot(flat, weights_ref[1, :, : 3 * LANES]).astype(BF)
+    qkv_two[...] = dot_nt(flat, weights_ref[1, : 3 * LANES]).astype(BF)
     attend_forward(heads, qkv_two, probs_two, attn_two, same)
     sum_blocks[1] = (
-        dot_nt(attn_two[...], weights_ref[1, :, 3 * LANES :]).reshape(4, quarter, width).astype(BF)
+        dot(attn_two[...], weights_ref[1, 3 * LANES :]).reshape(4, quarter, width).astype(BF)
     )
     ring_sums[1].start()
     ring_sums[1].middle()
@@ -506,10 +522,10 @@
     gathers[1].finish()
 
     flat = gather_blocks[1].reshape(rows, width)
-    dout_ref[...] = dot(flat, weights_ref[1, :, 3 * LANES :]).astype(BF)
+    dout_ref[...] = dot_nt(flat, weights_ref[1, 3 * LANES :]).astype(BF)
     attend_backward(heads, qkv_two, probs_two, dout_ref, dqkv_ref)
     sum_blocks[2] = (
-        dot_nt(dqkv_ref[...], weights_ref[1, :, : 3 * LANES])
+        dot(dqkv_ref[...], weights_ref[1, : 3 * LANES])
         .reshape(4, quarter, width)
         .astype(BF)
     )
@@ -564,7 +580,7 @@
 
     def finish_z(use):
         z_swaps[use].finish()
-        grads_out[1 - use] = jnp.sum(z_in[use].astype(F32), axis=0)
+        return jnp.sum(z_in[use].astype(F32), axis=0)
 
     reduce_pair(0)
     y_sums[0].start()
@@ -591,7 +607,7 @@
     gathers[2].finish()
 
     flat = gather_blocks[2].reshape(rows, width)
-    dout_ref[...] = dot(flat, weights_ref[0, :, 3 * LANES :]).astype(BF)
+    dout_ref[...] = dot_nt(flat, weights_ref[0, 3 * LANES :]).astype(BF)
     start_z(0)
     for copy in err_copies:
         copy.wait()
@@ -604,14 +620,19 @@
     compact_ref[...] = compact(dqkv_ref)
     weight_grads(input_one, compact_ref, View(2), attn_one, partial_ref.at[1], half_rows)
     pairs[1].start()
-    finish_z(0)
+    second_grads = finish_z(0)
     err_copy.wait()
-    errors_out[...] = err_pair[...]
+    margin = (err_pair[0] - err_pair[1]) * (1.0 / (rows * peers * width))
+    scaled = beta_dpo * (margin - (ref_losses[0] - ref_losses[1]))
+    loss_out[...] = jnp.maximum(scaled, 0.0) + jnp.log1p(jnp.exp(-jnp.abs(scaled)))
+    factor = (rows * peers * beta_dpo) * jax.nn.sigmoid(scaled)
+    factor = factor[:1, :1]
     reduce_pair(1)
     y_sums[1].start()
     y_sums[1].middle()
     start_z(1)
-    finish_z(1)
+    grads_out[1] = second_grads * factor
+    grads_out[0] = finish_z(1) * factor
 
 
 def local(latents, noise, timesteps, ref_losses, weights):
@@ -626,24 +647,22 @@
     out_rows = y_rows // planes
     z_rows = -(-out_rows // 8) * 8
     heads = columns // HEAD_DIM
-    tokens_total = rows * peers
 
     angle = (timesteps[0, 0].astype(F32) / 1000.0 + 0.008) / 1.008 * (math.pi / 2)
     plan = jnp.cos(angle) ** 2
     scales = jnp.stack([jnp.sqrt(plan), jnp.sqrt(1.0 - plan)])
-    padded = jnp.pad(weights, ((0, 0), (0, 0), (0, 0), (0, LANES - columns)))
-    padded = padded.transpose(1, 0, 2, 3).reshape(2, width, 4 * LANES)
 
     vmem = pltpu.VMEM
     dma = pltpu.SemaphoreType.DMA
     third = width // 3
-    grads, errors = pl.pallas_call(
+    grads, loss = pl.pallas_call(
         functools.partial(kernel, peers, heads),
         out_shape=(
             jax.ShapeDtypeStruct((2, z_rows, width), F32),
-            jax.ShapeDtypeStruct((2, 8, 128), F32),
+            jax.ShapeDtypeStruct((8, 128), F32),
         ),
         in_specs=[
+            pl.BlockSpec(memory_space=pltpu.SMEM),
             pl.BlockSpec(memory_space=pltpu.SMEM),
             pl.BlockSpec(memory_space=vmem),
             pl.BlockSpec(memory_space=vmem),
@@ -651,8 +670,8 @@
         ],
         out_specs=(pl.BlockSpec(memory_space=vmem), pl.BlockSpec(memory_space=vmem)),
         scratch_shapes=[
-            vmem((2, width, 4 * LANES), BF),
-            dma((2,)),
+            vmem((2, 4 * LANES, width), BF),
+            dma((2, 4)),
             vmem((rows, width), BF),
             vmem((rows, 3 * LANES), BF),
             vmem((rows, 3 * LANES), BF),
@@ -705,14 +724,10 @@
         compiler_params=pltpu.CompilerParams(
             collective_id=0, has_side_effects=True, vmem_limit_bytes=60 * 2**20
         ),
-    )(scales, latents[0, 0], noise[0, 0], padded)
-
-    errors = errors[:, 0, 0] / (tokens_total * width)
-    margin = errors[0] - ref_losses[0, 0] - (errors[1] - ref_losses[1, 0])
-    dpo_loss = jax.nn.softplus(beta_dpo * margin)
-    coefficient = tokens_total * beta_dpo * jax.nn.sigmoid(beta_dpo * margin)
+    )(scales, ref_losses[:, 0], latents[0, 0], noise[0, 0], weights.transpose(1, 2, 3, 0))
+
     grads = grads[:, :out_rows].reshape(2, out_rows, 4, columns).transpose(1, 0, 2, 3)
-    return (dpo_loss, grads * coefficient)
+    return (loss[0, 0], grads)
 
 
 def solution(mesh):

time: 146 us -> 126 us (0.86)
  local copies, waits for them, and re-layouts: 18.8 us -> 3.18 us
  between operations: 5.3 us -> 1.45 us
  other arithmetic: 2.26 us -> 0.65 us
    reshape x1, local copies, waits for them, and re-layouts: 10.3 us -> 0.96 us  [local(): grads[:, :out_rows].reshape(2, out_rows, 4, columns).transpose(1, 0, 2, 3)]
    pad x1 -> x0, local copies, waits for them, and re-layouts: 6.38 us -> none  [local(): padded = jnp.pad(weights, ((0, 0), (0, 0), (0, 0), (0, LANES - columns)))]
where the time goes in v2:
time: 126 us
  Pallas kernels  120 us (95%)
  local copies, waits for them, and re-layouts  3.18 us (3%)
  between operations  1.45 us (1%)
    pallas_call x1, Pallas kernels, local(): pl.pallas_call(functools.partial(kernel, peers, heads), out_shape=(jax.Sh...  120 us

profile of v2, /device:TPU:1, one launch (start us, length us, event | category | flops | bytes accessed | tf_op | source)
XLA Modules:
  0.0 125.5 jit_solution(6337496598402438436)
XLA Ops:
  1.4 0.6 pad_maximum_fusion.scale_ref
  2.1 120.2 %shard_map.68 = (f32[2,24,1152]{2,1,0:T(8,128)}, f32[8,128]{1,0:T(8,128)}) custom-call(f32[2]{0:T(128)} %pad_maximum_fusion.scale_ref, f32[2]{0:T(128)} %bitcast.16, bf16[256,1152]{1,0:T(8,128)(2,1)} %bitcast.12, bf16[256,1152]{1,0:T(8,128)(2,1)} %bitcast.13, bf16[2,4,288,1152]{3,2,1,0:T(8,128)(2,1)} %bitcast.11), custom_call_target="tpu_custom_call" | custom-call | tf_op jit(solution)/shard_map/pallas_call | solution.py:658
  122.3 1.2 slice.6
  123.5 1.0 copy.8
  124.6 1.0 reshape.14

commit v3 on v2

--- a/solution.py
+++ b/solution.py
@@ -153,7 +153,7 @@
     def __init__(self, blocks, low, high, send, recv, me, device, cut):
         self.blocks, self.low, self.high, self.me, self.cut = blocks, low, high, me, cut
         self.right, self.left = (me + 1) % 4, (me + 3) % 4
-        opposite = (me + 2) % 4
+        self.opposite = opposite = (me + 2) % 4
         rows = blocks.shape[1]
         self.lo, self.hi = pl.ds(0, cut), pl.ds(cut, rows - cut)
         right, left = device(self.right), device(self.left)
@@ -168,10 +168,14 @@
         self.sum_right = copy(self.right, self.lo, low.at[1], 4, right)
         self.sum_left = copy(self.left, self.hi, high.at[1], 5, left)
 
-    def start(self):
+    def start(self, fill=None):
+        if fill is not None:
+            fill(self.opposite, self.right)
         self.far_right.start()
         self.far_left.start()
         self.near_right.start()
+        if fill is not None:
+            fill(self.left, self.me)
         self.near_left.start()
 
     def middle(self):
@@ -202,7 +206,9 @@
 
 class RingGather:
     def __init__(self, blocks, send, recv, me, device):
+        self.blocks, self.me = blocks, me
         self.right, self.left = (me + 1) % 4, (me + 3) % 4
+        self.opposite = (me + 2) % 4
         half = blocks.shape[1] // 2
         lo, hi = pl.ds(0, half), pl.ds(half, half)
         right, left = device(self.right), device(self.left)
@@ -230,9 +236,21 @@
         self.first_left.wait_recv()
         self.pass_left.start()
 
-    def finish(self):
-        for copy in (self.next_right, self.next_left, self.pass_right, self.pass_left):
-            copy.wait_recv()
+    def project(self, weights, out_ref):
+        size = self.blocks.shape[1]
+        self.next_right.wait_recv()
+        self.next_left.wait_recv()
+        near = (self.me, self.left, self.right)
+        result = dot_nt(jnp.concatenate([self.blocks[block] for block in near], axis=0), weights)
+        for place, block in enumerate(near):
+            out_ref[pl.ds(pl.multiple_of(block * size, size), size), :] = result[
+                place * size : (place + 1) * size
+            ].astype(BF)
+        self.pass_right.wait_recv()
+        self.pass_left.wait_recv()
+        out_ref[pl.ds(pl.multiple_of(self.opposite * size, size), size), :] = dot_nt(
+            self.blocks[self.opposite], weights
+        ).astype(BF)
         for copy in (
             self.first_right,
             self.first_left,
@@ -454,6 +472,30 @@
     unpacking = [unpack_matrix(peers, tokens, third) for third in range(3)]
     clean_scale, noise_scale = scale_ref[0], scale_ref[1]
 
+    state = clean_scale * latent_ref[...].astype(F32) + noise_scale * noise_ref[...].astype(F32)
+    center = state - jnp.mean(state, axis=1, keepdims=True)
+    inv_std = lax.rsqrt(jnp.mean(center * center, axis=1, keepdims=True) + norm_eps)
+    input_one[...] = (center * inv_std).astype(BF)
+    for load in loads[0]:
+        load.wait()
+    qkv_one[...] = dot_nt(input_one[...], weights_ref[0, : 3 * LANES]).astype(BF)
+    attend_forward(heads, qkv_one, probs_one, attn_one, None)
+
+    def fill(use, rows_ref, weights):
+        def both(*blocks):
+            sources = [
+                rows_ref[pl.ds(pl.multiple_of(block * quarter, quarter), quarter), :]
+                for block in blocks
+            ]
+            result = dot(jnp.concatenate(sources, axis=0), weights)
+            for place, block in enumerate(blocks):
+                sum_blocks[use, block] = result[place * quarter : (place + 1) * quarter].astype(BF)
+
+        return both
+
+    pl.semaphore_wait(barrier, peers + 3)
+    ring_sums[0].start(fill(0, attn_one, weights_ref[0, 3 * LANES :]))
+
     mine = pl.ds(pl.multiple_of(x * quarter, quarter), quarter)
     first_out[...] = jnp.concatenate(
         [
@@ -462,21 +504,8 @@
         ],
         axis=1,
     ).astype(BF)
-    pl.semaphore_wait(barrier, peers + 3)
     first.start()
 
-    state = clean_scale * latent_ref[...].astype(F32) + noise_scale * noise_ref[...].astype(F32)
-    center = state - jnp.mean(state, axis=1, keepdims=True)
-    inv_std = lax.rsqrt(jnp.mean(center * center, axis=1, keepdims=True) + norm_eps)
-    input_one[...] = (center * inv_std).astype(BF)
-    for load in loads[0]:
-        load.wait()
-    qkv_one[...] = dot_nt(input_one[...], weights_ref[0, : 3 * LANES]).astype(BF)
-    attend_forward(heads, qkv_one, probs_one, attn_one, None)
-    sum_blocks[0] = (
-        dot(attn_one[...], weights_ref[0, 3 * LANES :]).reshape(4, quarter, width).astype(BF)
-    )
-    ring_sums[0].start()
     ring_sums[0].middle()
     out_one = ring_sums[0].finish()
 
@@ -496,20 +525,14 @@
     gather_blocks[0, x] = norm_ref[...].astype(BF)
     gathers[0].start()
     gathers[0].middle()
-    gathers[0].finish()
-
-    input_two = gather_blocks.at[0]
+
     for load in loads[1]:
         load.wait()
     row, col = iota((rows, rows), 0), iota((rows, rows), 1)
     same = (row // quarter == col // quarter) & (row % tokens == col % tokens)
-    flat = input_two[...].reshape(rows, width)
-    qkv_two[...] = dot_nt(flat, weights_ref[1, : 3 * LANES]).astype(BF)
+    gathers[0].project(weights_ref[1, : 3 * LANES], qkv_two)
     attend_forward(heads, qkv_two, probs_two, attn_two, same)
-    sum_blocks[1] = (
-        dot(attn_two[...], weights_ref[1, 3 * LANES :]).reshape(4, quarter, width).astype(BF)
-    )
-    ring_sums[1].start()
+    ring_sums[1].start(fill(1, attn_two, weights_ref[1, 3 * LANES :]))
     ring_sums[1].middle()
     diff = state_ref[...] + ring_sums[1].finish() - noise_pos[...]
     error = jnp.sum(jnp.sum(diff * diff, axis=1, keepdims=True), axis=0, keepdims=True)
@@ -519,17 +542,10 @@
     gather_blocks[1, x] = grad.astype(BF)
     gathers[1].start()
     gathers[1].middle()
-    gathers[1].finish()
-
-    flat = gather_blocks[1].reshape(rows, width)
-    dout_ref[...] = dot_nt(flat, weights_ref[1, 3 * LANES :]).astype(BF)
+
+    gathers[1].project(weights_ref[1, 3 * LANES :], dout_ref)
     attend_backward(heads, qkv_two, probs_two, dout_ref, dqkv_ref)
-    sum_blocks[2] = (
-        dot(dqkv_ref[...], weights_ref[1, : 3 * LANES])
-        .reshape(4, quarter, width)
-        .astype(BF)
-    )
-    ring_sums[2].start()
+    ring_sums[2].start(fill(2, dqkv_ref, weights_ref[1, : 3 * LANES]))
     compact_ref[...] = compact(dqkv_ref)
     ring_sums[2].middle()
 
@@ -604,35 +620,31 @@
         copy.start()
     gathers[2].middle()
     y_sums[0].middle()
-    gathers[2].finish()
-
-    flat = gather_blocks[2].reshape(rows, width)
-    dout_ref[...] = dot_nt(flat, weights_ref[0, 3 * LANES :]).astype(BF)
-    start_z(0)
+
+    gathers[2].project(weights_ref[0, 3 * LANES :], dout_ref)
     for copy in err_copies:
         copy.wait()
     err_pair[pair] = jnp.sum(err_x[...], axis=0)
-    err_copy = remote(
-        err_pair.at[pair], err_pair.at[pair], err_pair_send, err_pair_recv, other
-    )
+    err_copy = remote(err_pair.at[pair], err_pair.at[pair], err_pair_send, err_pair_recv, other)
     err_copy.start()
     attend_backward(heads, qkv_one, probs_one, dout_ref, dqkv_ref)
     compact_ref[...] = compact(dqkv_ref)
     weight_grads(input_one, compact_ref, View(2), attn_one, partial_ref.at[1], half_rows)
     pairs[1].start()
-    second_grads = finish_z(0)
+    start_z(0)
+    reduce_pair(1)
+    y_sums[1].start()
     err_copy.wait()
     margin = (err_pair[0] - err_pair[1]) * (1.0 / (rows * peers * width))
     scaled = beta_dpo * (margin - (ref_losses[0] - ref_losses[1]))
-    loss_out[...] = jnp.maximum(scaled, 0.0) + jnp.log1p(jnp.exp(-jnp.abs(scaled)))
+    loss = jnp.maximum(scaled, 0.0) + jnp.log1p(jnp.exp(-jnp.abs(scaled)))
+    loss_out[0, 0] = loss[0, 0]
     factor = (rows * peers * beta_dpo) * jax.nn.sigmoid(scaled)
     factor = factor[:1, :1]
-    reduce_pair(1)
-    y_sums[1].start()
     y_sums[1].middle()
+    grads_out[:, 1, :] = (finish_z(0) * factor)[:out_rows]
     start_z(1)
-    grads_out[1] = second_grads * factor
-    grads_out[0] = finish_z(1) * factor
+    grads_out[:, 0, :] = (finish_z(1) * factor)[:out_rows]
 
 
 def local(latents, noise, timesteps, ref_losses, weights):
@@ -658,8 +670,8 @@
     grads, loss = pl.pallas_call(
         functools.partial(kernel, peers, heads),
         out_shape=(
-            jax.ShapeDtypeStruct((2, z_rows, width), F32),
-            jax.ShapeDtypeStruct((8, 128), F32),
+            jax.ShapeDtypeStruct((out_rows, 2, width), F32),
+            jax.ShapeDtypeStruct((1, 1), F32),
         ),
         in_specs=[
             pl.BlockSpec(memory_space=pltpu.SMEM),
@@ -668,7 +680,7 @@
             pl.BlockSpec(memory_space=vmem),
             pl.BlockSpec(memory_space=pl.ANY),
         ],
-        out_specs=(pl.BlockSpec(memory_space=vmem), pl.BlockSpec(memory_space=vmem)),
+        out_specs=(pl.BlockSpec(memory_space=vmem), pl.BlockSpec(memory_space=pltpu.SMEM)),
         scratch_shapes=[
             vmem((2, 4 * LANES, width), BF),
             dma((2, 4)),
@@ -726,8 +738,7 @@
         ),
     )(scales, ref_losses[:, 0], latents[0, 0], noise[0, 0], weights.transpose(1, 2, 3, 0))
 
-    grads = grads[:, :out_rows].reshape(2, out_rows, 4, columns).transpose(1, 0, 2, 3)
-    return (loss[0, 0], grads)
+    return (loss[0, 0], grads.reshape(out_rows, 2, 4, columns))
 
 
 def solution(mesh):

time: 126 us -> 124 us (0.984)
  Pallas kernels: 120 us -> 117 us
  between operations: 1.45 us -> 3.21 us
  local copies, waits for them, and re-layouts: 3.18 us -> 1.88 us
    pallas_call x1, Pallas kernels: 120 us -> 117 us  [local(): pl.pallas_call(functools.partial(kernel, peers, heads), out_shape=(jax.Sh...]
    slice x2 -> x0, local copies, waits for them, and re-layouts: 2.21 us -> none  [the longest x1 1.19 us: local(): return (loss[0, 0], grads)]
where the time goes in v3:
time: 124 us; the launch traced here: 122 us
  Pallas kernels  117 us (94%)
  between operations  3.21 us (3%)
  local copies, waits for them, and re-layouts  1.88 us (2%)
    pallas_call x1, Pallas kernels, local(): pl.pallas_call(functools.partial(kernel, peers, heads), out_shape=(jax.Sh...  117 us

profile of v3, /device:TPU:1, one launch (start us, length us, event | category | flops | bytes accessed | tf_op | source)
XLA Modules:
  0.0 122.4 jit_solution(16511163781422069235)
XLA Ops:
  1.4 0.6 pad_maximum_fusion.scale_ref
  2.1 116.7 %shard_map.68 = (f32[18,2,1152]{2,1,0:T(2,128)}, f32[1,1]{1,0:T(1,128)}) custom-call(f32[2]{0:T(128)} %pad_maximum_fusion.scale_ref, f32[2]{0:T(128)} %bitcast.10, bf16[256,1152]{1,0:T(8,128)(2,1)} %bitcast.8, bf16[256,1152]{1,0:T(8,128)(2,1)} %bitcast.9, bf16[2,4,288,1152]{3,2,1,0:T(8,128)(2,1)} %bitcast.7), custom_call_target="tpu_custom_call" | custom-call | tf_op jit(solution)/shard_map/pallas_call | solution.py:670
  118.8 1.9 %reshape.14 = f32[18,2,4,288]{3,2,1,0:T(4,128)} reshape(f32[18,2,1152]{2,1,0:T(2,128)} %get-tuple-element.5) | data formatting | bytes 331776 | tf_op jit(solution)/shard_map/reshape | solution.py:741

commit v4 on v3

v4 whole, which is shorter than its diff:
```python
import functools
import math

import jax
import jax.numpy as jnp
from jax import lax
from jax.experimental import pallas as pl
from jax.experimental.pallas import tpu as pltpu
from jax.sharding import PartitionSpec as P

HEAD_DIM = 72
LANES = 384
NY = 4
MESH = pl.DeviceIdType.MESH
BF = jnp.bfloat16
F32 = jnp.float32

beta_dpo = 0.5
norm_eps = 1e-06


def dot(a, b):
    return jnp.dot(a, b, preferred_element_type=F32)


def dot_nt(a, b):
    return lax.dot_general(a, b, (((1,), (1,)), ((), ())), preferred_element_type=F32)


def dot_tn(a, b):
    return lax.dot_general(a, b, (((0,), (0,)), ((), ())), preferred_element_type=F32)


def iota(shape, axis):
    return lax.broadcasted_iota(jnp.int32, shape, axis)


def head_mask(head, dtype):
    lane = iota((1, LANES), 1)
    return ((lane >= head * HEAD_DIM) & (lane < (head + 1) * HEAD_DIM)).astype(dtype)


def attend_forward(heads, qkv_ref, probs_ref, out_ref, mask):
    queries = qkv_ref[:, :LANES]
    keys = qkv_ref[:, LANES : 2 * LANES]
    values = qkv_ref[:, 2 * LANES :]
    total = None
    for head in range(heads):
        scores = dot_nt(queries * head_mask(head, BF), keys) * (HEAD_DIM**-0.5)
        if mask is not None:
            scores = jnp.where(mask, scores, -1e30)
        scores = jnp.exp(scores - jnp.max(scores, axis=1, keepdims=True))
        probs = scores * (1.0 / jnp.sum(scores, axis=1, keepdims=True))
        probs_ref[head] = probs
        part = dot(probs.astype(BF), values) * head_mask(head, F32)
        total = part if total is None else total + part
    out_ref[...] = total.astype(BF)


def values_backward(heads, probs_ref, grad_ref, dqkv_ref):
    grad = grad_ref[...]
    total = None
    for head in range(heads):
        part = dot_tn(probs_ref[head].astype(BF), grad) * head_mask(head, F32)
        total = part if total is None else total + part
    dqkv_ref[:, 2 * LANES :] = total.astype(BF)


def scores_backward(heads, qkv_ref, probs_ref, grad_ref, dqkv_ref):
    queries = qkv_ref[:, :LANES]
    keys = qkv_ref[:, LANES : 2 * LANES]
    values = qkv_ref[:, 2 * LANES :]
    grad = grad_ref[...]
    sums = [None, None]
    for head in range(heads):
        probs = probs_ref[head]
        dprobs = dot_nt(grad * head_mask(head, BF), values)
        delta = jnp.sum(dprobs * probs, axis=1, keepdims=True)
        dscores = (probs * (dprobs - delta) * (HEAD_DIM**-0.5)).astype(BF)
        parts = (dot(dscores, keys), dot_tn(dscores, queries))
        for slot in range(2):
            part = parts[slot] * head_mask(head, F32)
            sums[slot] = part if sums[slot] is None else sums[slot] + part
    for slot in range(2):
        dqkv_ref[:, slot * LANES : (slot + 1) * LANES] = sums[slot].astype(BF)


def beside(first, second):
    return jnp.concatenate(
        [first[:, :256], first[:, 256:] + second[:, :128], second[:, 128:]], axis=1
    )


def shifted(values, lanes):
    return pltpu.roll(values.astype(F32), lanes, 1)


def store_rows(out_ref, start, rows, half_rows):
    done, count = 0, rows.shape[0]
    while done < count:
        half, at = divmod(start + done, half_rows)
        size = min(count - done, half_rows - at)
        out_ref[half, at : at + size, :] = rows[done : done + size].astype(BF)
        done += size


def pack_matrix(peers, tokens):
    shape = (8 * peers, 3 * peers * tokens)
    row, col = iota(shape, 0), iota(shape, 1)
    peer, inner = row // 8, row % 8
    source = (inner // tokens) * (peers * tokens) + peer * tokens + inner % tokens
    return ((inner < 3 * tokens) & (col == source)).astype(F32).astype(BF)


def unpack_matrix(peers, tokens, third):
    shape = (peers * tokens, 8 * peers)
    token, col = iota(shape, 0), iota(shape, 1)
    source = (token // tokens) * 8 + third * tokens + token % tokens
    return (col == source).astype(F32).astype(BF)


def pack(rows, matrix, peers):
    third = rows.shape[1] // 3
    stacked = jnp.concatenate(
        [rows[:, :third], rows[:, third : 2 * third], rows[:, 2 * third :]], axis=0
    )
    return dot(matrix, stacked).reshape(peers, 8, third)


def unpack(messages, matrices, peers):
    flat = messages.reshape(8 * peers, messages.shape[2]).astype(BF)
    return jnp.concatenate([dot(matrix, flat) for matrix in matrices], axis=1)


def remote(src, dst, send, recv, device):
    return pltpu.make_async_remote_copy(
        src_ref=src,
        dst_ref=dst,
        send_sem=send,
        recv_sem=recv,
        device_id=device,
        device_id_type=MESH,
    )


def halves(rows):
    unit = 16 if rows >= 64 else rows // 4
    cut = -(-rows // (2 * unit)) * unit
    low, high = -(-cut // (2 * unit)) * unit, -(-(rows - cut) // (2 * unit)) * unit
    return (
        cut,
        ((0, low), (low, cut - low)),
        ((cut, high), (cut + high, rows - cut - high)),
    )


class RingGather:
    def __init__(self, blocks, send, recv, me, device):
        self.blocks, self.me = blocks, me
        self.right, self.left = (me + 1) % 4, (me + 3) % 4
        self.opposite = (me + 2) % 4
        rows = blocks.shape[1]
        cut, lows, highs = halves(rows)
        right, left = device(self.right), device(self.left)

        def copy(block, piece, index, to):
            ref = blocks.at[block, pl.ds(*piece)]
            return remote(ref, ref, send.at[index], recv.at[index], to)

        self.first, self.passes = [], []
        for place, piece in enumerate(lows):
            self.first.append(copy(me, piece, place, right))
            self.passes.append(copy(self.left, piece, 4 + place, right))
        for place, piece in enumerate(highs):
            self.first.append(copy(me, piece, 2 + place, left))
            self.passes.append(copy(self.right, piece, 6 + place, left))
        self.next_right = copy(me, (cut, rows - cut), 8, right)
        self.next_left = copy(me, (0, cut), 9, left)

    def start(self):
        for place in (0, 2, 1, 3):
            self.first[place].start()
        self.next_right.start()
        self.next_left.start()

    def middle(self):
        for place in (0, 2, 1, 3):
            self.first[place].wait_recv()
            self.passes[place].start()

    def project(self, weights, out_ref):
        size = self.blocks.shape[1]
        self.next_right.wait_recv()
        self.next_left.wait_recv()
        near = (self.me, self.left, self.right)
        result = dot_nt(jnp.concatenate([self.blocks[block] for block in near], axis=0), weights)
        for place, block in enumerate(near):
            out_ref[pl.ds(pl.multiple_of(block * size, size), size), :] = result[
                place * size : (place + 1) * size
            ].astype(BF)
        for copy in self.passes:
            copy.wait_recv()
        out_ref[pl.ds(pl.multiple_of(self.opposite * size, size), size), :] = dot_nt(
            self.blocks[self.opposite], weights
        ).astype(BF)
        for copy in self.first + self.passes + [self.next_right, self.next_left]:
            copy.wait_send()


class Exchange:
    def __init__(self, out, into, send, recv, me, peers):
        self.out, self.into, self.me, self.peers = out, into, me, peers
        self.copies = [
            remote(out.at[peer], into.at[me], send, recv, device) for peer, device in peers
        ]
        every = pl.ds(0, len(peers))
        self.all = remote(out.at[every], into.at[every], send, recv, peers[0][1])

    def start(self):
        for copy in self.copies:
            copy.start()

    def keep(self):
        self.into[self.me] = self.out[self.me]

    def finish(self):
        self.all.wait()


class Total:
    def __init__(self, refs, pair, other, y, y_peers, z, z_peers):
        self.partial, self.pair_in, y_out, y_in, z_out, z_in, sems = refs
        self.pair = pair
        self.swap = remote(self.partial.at[1 - pair], self.pair_in, sems.at[0], sems.at[1], other)
        self.over_y = Exchange(y_out, y_in, sems.at[2], sems.at[3], y, y_peers)
        self.over_z = Exchange(z_out, z_in, sems.at[4], sems.at[5], z, z_peers)

    def start(self):
        self.swap.start()

    def start_y(self):
        self.swap.wait()
        step = self.over_y
        rows = step.out.shape[1]

        def fill(block):
            at = pl.ds(pl.multiple_of(block * rows, 16), rows)
            own = self.partial[self.pair, at, :].astype(F32) + self.pair_in[at, :].astype(F32)
            step.out[block] = own.astype(BF)

        for (block, _), copy in zip(step.peers, step.copies):
            fill(block)
            copy.start()
        fill(step.me)
        step.keep()

    def start_z(self, spread):
        self.over_y.finish()
        rows = jnp.sum(self.over_y.into[...].astype(F32), axis=0).astype(BF)
        step = self.over_z
        step.out[...] = dot(spread, rows).reshape(step.out.shape).astype(BF)
        step.start()
        step.keep()

    def finish(self):
        self.over_z.finish()
        return jnp.sum(self.over_z.into[...].astype(F32), axis=0)


def kernel(
    peers,
    heads,
    scale_ref,
    ref_losses,
    latent_ref,
    noise_ref,
    weights_hbm,
    grads_out,
    loss_out,
    weights_ref,
    weights_sem,
    input_one,
    qkv_one,
    qkv_two,
    probs_one,
    probs_two,
    attn_one,
    attn_two,
    dout_ref,
    dqkv_ref,
    start_pos,
    noise_pos,
    state_ref,
    norm_ref,
    grad_ref,
    sum_out,
    sum_in,
    sum_send,
    sum_recv,
    gather_blocks,
    gather_send,
    gather_recv,
    first_out,
    first_in,
    swap_out,
    swap_in,
    swap_send,
    swap_recv,
    err_x,
    err_x_send,
    err_x_recv,
    err_pair,
    err_pair_send,
    err_pair_recv,
    *total_refs,
):
    pair, seq, x = lax.axis_index("pair"), lax.axis_index("seq"), lax.axis_index("tensor")
    planes = peers // NY
    y, z = seq // planes, seq % planes
    rows, width = latent_ref.shape
    quarter = rows // 4
    tokens = quarter // peers
    half_rows = width // 2
    y_rows = half_rows // NY
    out_rows = y_rows // planes
    z_rows = total_refs[4].shape[1]

    def at_x(index):
        return (pair, seq, index)

    def at_y(index):
        return (pair, index * planes + z, x)

    def at_z(index):
        return (pair, y * planes + index, x)

    def at_seq(index):
        return (pair, index, x)

    other = (1 - pair, seq, x)

    columns = weights_hbm.shape[2]
    loads = [
        [
            pltpu.make_async_copy(
                weights_hbm.at[block, slot],
                weights_ref.at[block, pl.ds(slot * LANES, columns)],
                weights_sem.at[block, slot],
            )
            for slot in range(4)
        ]
        for block in range(2)
    ]
    for load in loads[0] + loads[1]:
        load.start()
    for slot in range(4):
        for block in range(2):
            weights_ref[block, slot * LANES + columns : (slot + 1) * LANES, :] = jnp.zeros(
                (LANES - columns, width), BF
            )

    barrier = pltpu.get_barrier_semaphore()

    def greet(offset, carry):
        pl.semaphore_signal(
            barrier, inc=1, device_id=at_seq((seq + offset) % peers), device_id_type=MESH
        )
        return carry

    lax.fori_loop(1, peers, greet, 0)
    for offset in range(1, 4):
        pl.semaphore_signal(
            barrier, inc=1, device_id=at_x((x + offset) % 4), device_id_type=MESH
        )
    pl.semaphore_signal(barrier, inc=1, device_id=other, device_id_type=MESH)

    def hops(offset, count):
        return min(offset, count - offset)

    x_peers = [((x + offset) % 4, at_x((x + offset) % 4)) for offset in (2, 1, 3)]
    y_peers = [((y + offset) % NY, at_y((y + offset) % NY)) for offset in (2, 1, 3)]
    z_order = sorted(range(1, planes), key=lambda offset: -hops(offset, planes))
    z_peers = [((z + offset) % planes, at_z((z + offset) % planes)) for offset in z_order]
    order = sorted(
        ((dy, dz) for dy in range(NY) for dz in range(planes) if dy or dz),
        key=lambda offset: -hops(offset[0], NY) - hops(offset[1], planes),
    )
    seq_peers = []
    for dy, dz in order:
        peer = ((y + dy) % NY) * planes + (z + dz) % planes
        seq_peers.append((peer, at_seq(peer)))

    sums = [
        Exchange(
            sum_out.at[use], sum_in.at[use], sum_send.at[use], sum_recv.at[use], x, x_peers
        )
        for use in range(3)
    ]
    gathers = [
        RingGather(gather_blocks.at[use], gather_send.at[use], gather_recv.at[use], x, at_x)
        for use in range(3)
    ]
    first = Exchange(first_out, first_in, swap_send.at[0], swap_recv.at[0], seq, seq_peers)
    swaps = [
        Exchange(
            swap_out.at[use],
            swap_in.at[use],
            swap_send.at[use + 1],
            swap_recv.at[use + 1],
            seq,
            seq_peers,
        )
        for use in range(2)
    ]
    total_two, total_values, total_queries, total_keys = [
        Total(total_refs[7 * use : 7 * use + 7], pair, other, y, y_peers, z, z_peers)
        for use in range(4)
    ]

    packing = pack_matrix(peers, tokens)
    unpacking = [unpack_matrix(peers, tokens, third) for third in range(3)]
    clean_scale, noise_scale = scale_ref[0], scale_ref[1]

    state = clean_scale * latent_ref[...].astype(F32) + noise_scale * noise_ref[...].astype(F32)
    center = state - jnp.mean(state, axis=1, keepdims=True)
    inv_std = lax.rsqrt(jnp.mean(center * center, axis=1, keepdims=True) + norm_eps)
    input_one[...] = (center * inv_std).astype(BF)
    for load in loads[0]:
        load.wait()
    qkv_one[...] = dot_nt(input_one[...], weights_ref[0, : 3 * LANES]).astype(BF)
    attend_forward(heads, qkv_one, probs_one, attn_one, None)

    def sum_start(use, rows_ref, weights):
        step = sums[use]
        (opposite, _), (right, _), (left, _) = step.peers
        for blocks in ((opposite, right), (left, x)):
            sources = [
                rows_ref[pl.ds(pl.multiple_of(block * quarter, quarter), quarter), :]
                for block in blocks
            ]
            result = dot(jnp.concatenate(sources, axis=0), weights)
            for place, block in enumerate(blocks):
                step.out[block] = result[place * quarter : (place + 1) * quarter].astype(BF)
            if blocks[0] is opposite:
                step.copies[0].start()
                step.copies[1].start()
            else:
                step.copies[2].start()

    def sum_finish(use):
        step = sums[use]
        step.finish()
        total = step.out[x].astype(F32)
        for peer, _ in step.peers:
            total = total + step.into[peer].astype(F32)
        return total

    pl.semaphore_wait(barrier, peers + 3)
    sum_start(0, attn_one, weights_ref[0, 3 * LANES :])

    mine = pl.ds(pl.multiple_of(x * quarter, quarter), quarter)
    first_out[...] = jnp.concatenate(
        [
            pack(latent_ref[mine, :], packing, peers),
            pack(noise_ref[mine, :], packing, peers),
        ],
        axis=1,
    ).astype(BF)
    first.start()
    first.keep()

    out_one = sum_finish(0)

    swap_out[0] = pack(out_one.astype(BF), packing, peers).astype(BF)
    swaps[0].start()
    swaps[0].keep()
    first.finish()
    messages = first_in[...].astype(F32)
    clean = unpack(messages[:, :8], unpacking, peers)
    noise_pos[...] = unpack(messages[:, 8:], unpacking, peers)
    start_pos[...] = clean_scale * clean + noise_scale * noise_pos[...]
    swaps[0].finish()
    state = start_pos[...] + unpack(swap_in[0].astype(F32), unpacking, peers)
    state_ref[...] = state
    center = state - jnp.mean(state, axis=1, keepdims=True)
    inv_two = lax.rsqrt(jnp.mean(center * center, axis=1, keepdims=True) + norm_eps)
    norm_ref[...] = center * inv_two
    gather_blocks[0, x] = norm_ref[...].astype(BF)
    gathers[0].start()
    gathers[0].middle()

    for load in loads[1]:
        load.wait()
    row, col = iota((rows, rows), 0), iota((rows, rows), 1)
    same = (row // quarter == col // quarter) & (row % tokens == col % tokens)
    gathers[0].project(weights_ref[1, : 3 * LANES], qkv_two)
    attend_forward(heads, qkv_two, probs_two, attn_two, same)
    sum_start(1, attn_two, weights_ref[1, 3 * LANES :])
    diff = state_ref[...] + sum_finish(1) - noise_pos[...]
    error = jnp.sum(jnp.sum(diff * diff, axis=1, keepdims=True), axis=0, keepdims=True)
    sign = 1.0 - 2.0 * pair.astype(F32)
    grad = diff * (2.0 * sign / width)
    grad_ref[...] = grad
    gather_blocks[1, x] = grad.astype(BF)
    gathers[1].start()
    gathers[1].middle()

    gathers[1].project(weights_ref[1, 3 * LANES :], dout_ref)
    scores_backward(heads, qkv_two, probs_two, dout_ref, dqkv_ref)
    values_backward(heads, probs_two, dout_ref, dqkv_ref)
    sum_start(2, dqkv_ref, weights_ref[1, : 3 * LANES])

    def view(use, start, size):
        return gather_blocks[use, :, :, start : start + size].reshape(rows, size)

    step = 128
    shifted_keys = shifted(dqkv_ref[:, LANES : 2 * LANES], 32)
    shifted_values = shifted(dqkv_ref[:, 2 * LANES :], 64)
    queries_keys = beside(dqkv_ref[:, :LANES].astype(F32), shifted_keys)
    dqkv = jnp.concatenate(
        [
            queries_keys[:, :512],
            queries_keys[:, 512:] + shifted_values[:, :128],
            shifted_values[:, 128:],
        ],
        axis=1,
    ).astype(BF)
    attn = shifted(attn_two[...], 96).astype(BF)
    for start in range(0, width, step):
        first_part = dot_tn(view(0, start, step), dqkv)
        second_part = dot_tn(view(1, start, step), attn)
        block = jnp.concatenate(
            [
                first_part[:, :768],
                first_part[:, 768:] + second_part[:, :128],
                second_part[:, 128:],
            ],
            axis=1,
        )
        store_rows(total_two.partial, start, block, half_rows)
    total_two.start()
    dnorm = sum_finish(2)
    normed = norm_ref[...]
    mean_grad = jnp.mean(dnorm, axis=1, keepdims=True)
    mean_prod = jnp.mean(dnorm * normed, axis=1, keepdims=True)
    dstate = grad_ref[...] + inv_two * (dnorm - mean_grad - normed * mean_prod)

    messages = pack(dstate.astype(BF), packing, peers)
    inner = iota(messages.shape, 1)
    error_high = error.astype(BF).astype(F32)
    error_low = error - error_high
    messages = jnp.where(inner == 6, error_high.reshape(1, 1, 1), messages)
    messages = jnp.where(inner == 7, error_low.reshape(1, 1, 1), messages)
    swap_out[1] = messages.astype(BF)
    swaps[1].start()
    swaps[1].keep()

    shape = (planes * z_rows, y_rows)
    row, col = iota(shape, 0), iota(shape, 1)
    spread = (row % z_rows < out_rows) & (col == (row // z_rows) * out_rows + row % z_rows)
    spread = spread.astype(F32).astype(BF)

    total_two.start_y()
    swaps[1].finish()
    messages = swap_in[1].astype(F32)
    gather_blocks[2, x] = unpack(messages, unpacking, peers).astype(BF)
    gathers[2].start()
    total = jnp.sum(messages, axis=0)
    err_x[x] = jnp.broadcast_to(total[6:7, :128] + total[7:8, :128], (8, 128))
    err_copies = [
        remote(
            err_x.at[x],
            err_x.at[x],
            err_x_send.at[offset - 1],
            err_x_recv.at[offset - 1],
            at_x((x + offset) % 4),
        )
        for offset in range(1, 4)
    ]
    for copy in err_copies:
        copy.start()
    gathers[2].middle()

    gathers[2].project(weights_ref[0, 3 * LANES :], dout_ref)
    values_backward(heads, probs_one, dout_ref, dqkv_ref)
    values = dqkv_ref[:, 2 * LANES :]
    attn = shifted(attn_one[...], 32).astype(BF)
    for start in range(0, width, step):
        block = beside(
            dot_tn(input_one[:, start : start + step], values),
            dot_tn(view(2, start, step), attn),
        )
        store_rows(total_values.partial, start, block, half_rows)
    total_values.start()
    total_two.start_z(spread)
    for copy in err_copies:
        copy.wait()
    err_pair[pair] = jnp.sum(err_x[...], axis=0)
    err_copy = remote(err_pair.at[pair], err_pair.at[pair], err_pair_send, err_pair_recv, other)
    err_copy.start()
    total_values.start_y()
    scores_backward(heads, qkv_one, probs_one, dout_ref, dqkv_ref)
    queries_keys = beside(
        dqkv_ref[:, :LANES].astype(F32), shifted(dqkv_ref[:, LANES : 2 * LANES], 32)
    ).astype(BF)
    for start in range(0, width, step):
        block = dot_tn(input_one[:, start : start + step], queries_keys)
        store_rows(total_queries.partial, start, block[:, :LANES], half_rows)
        store_rows(total_keys.partial, start, block[:, LANES:], half_rows)
    total_queries.start()
    total_keys.start()
    err_copy.wait()
    margin = (err_pair[0] - err_pair[1]) * (1.0 / (rows * peers * width))
    scaled = beta_dpo * (margin - (ref_losses[0] - ref_losses[1]))
    loss = jnp.maximum(scaled, 0.0) + jnp.log1p(jnp.exp(-jnp.abs(scaled)))
    loss_out[0, 0] = loss[0, 0]
    factor = (rows * peers * beta_dpo) * jax.nn.sigmoid(scaled)
    factor = factor[:1, :1]
    total_queries.start_y()
    total_keys.start_y()
    grads_out[:, 1, :] = (total_two.finish() * factor)[:out_rows]
    total_values.start_z(spread)
    total_queries.start_z(spread)
    total_keys.start_z(spread)
    values_output = pltpu.roll(total_values.finish(), 64, 1)
    queries = total_queries.finish()
    keys = total_keys.finish()
    grads = jnp.concatenate(
        [
            queries,
            keys[:, :128],
            keys[:, 128:] + values_output[:, :128],
            values_output[:, 128:],
        ],
        axis=1,
    )
    grads_out[:, 0, :] = (grads * factor)[:out_rows]


def local(latents, noise, timesteps, ref_losses, weights):
    width, columns = weights.shape[0], weights.shape[3]
    rows = latents.shape[2]
    peers = lax.axis_size("seq")
    quarter = rows // 4
    planes = peers // NY
    half_rows = width // 2
    y_rows = half_rows // NY
    out_rows = y_rows // planes
    z_rows = -(-out_rows // 8) * 8
    heads = columns // HEAD_DIM

    angle = (timesteps[0, 0].astype(F32) / 1000.0 + 0.008) / 1.008 * (math.pi / 2)
    plan = jnp.cos(angle) ** 2
    scales = jnp.stack([jnp.sqrt(plan), jnp.sqrt(1.0 - plan)])

    vmem = pltpu.VMEM
    dma = pltpu.SemaphoreType.DMA
    third = width // 3
    totals = []
    for lanes in (width, 640, LANES, 256):
        totals += [
            vmem((2, half_rows, lanes), BF),
            vmem((half_rows, lanes), BF),
            vmem((NY, y_rows, lanes), BF),
            vmem((NY, y_rows, lanes), BF),
            vmem((planes, z_rows, lanes), BF),
            vmem((planes, z_rows, lanes), BF),
            dma((6,)),
        ]
    grads, loss = pl.pallas_call(
        functools.partial(kernel, peers, heads),
        out_shape=(
            jax.ShapeDtypeStruct((out_rows, 2, width), F32),
            jax.ShapeDtypeStruct((1, 1), F32),
        ),
        in_specs=[
            pl.BlockSpec(memory_space=pltpu.SMEM),
            pl.BlockSpec(memory_space=pltpu.SMEM),
            pl.BlockSpec(memory_space=vmem),
            pl.BlockSpec(memory_space=vmem),
            pl.BlockSpec(memory_space=pl.ANY),
        ],
        out_specs=(pl.BlockSpec(memory_space=vmem), pl.BlockSpec(memory_space=pltpu.SMEM)),
        scratch_shapes=[
            vmem((2, 4 * LANES, width), BF),
            dma((2, 4)),
            vmem((rows, width), BF),
            vmem((rows, 3 * LANES), BF),
            vmem((rows, 3 * LANES), BF),
            vmem((heads, rows, rows), F32),
            vmem((heads, rows, rows), F32),
            vmem((rows, LANES), BF),
            vmem((rows, LANES), BF),
            vmem((rows, LANES), BF),
            vmem((rows, 3 * LANES), BF),
            vmem((quarter, width), F32),
            vmem((quarter, width), F32),
            vmem((quarter, width), F32),
            vmem((quarter, width), F32),
            vmem((quarter, width), F32),
            vmem((3, 4, quarter, width), BF),
            vmem((3, 4, quarter, width), BF),
            dma((3,)),
            dma((3,)),
            vmem((3, 4, quarter, width), BF),
            dma((3, 10)),
            dma((3, 10)),
            vmem((peers, 16, third), BF),
            vmem((peers, 16, third), BF),
            vmem((2, peers, 8, third), BF),
            vmem((2, peers, 8, third), BF),
            dma((3,)),
            dma((3,)),
            vmem((4, 8, 128), F32),
            dma((3,)),
            dma((3,)),
            vmem((2, 8, 128), F32),
            dma,
            dma,
            *totals,
        ],
        compiler_params=pltpu.CompilerParams(
            collective_id=0, has_side_effects=True, vmem_limit_bytes=60 * 2**20
        ),
    )(scales, ref_losses[:, 0], latents[0, 0], noise[0, 0], weights.transpose(1, 2, 3, 0))

    return (loss[0, 0], grads.reshape(out_rows, 2, 4, columns))


def solution(mesh):
    in_specs = (
        P("pair", None, "seq", None),
        P("pair", None, "seq", None),
        P("pair", None),
        P(),
        P(None, None, None, "tensor"),
    )
    out_specs = (P(), P(("pair", "seq"), None, None, "tensor"))
    return jax.shard_map(local, mesh=mesh, in_specs=in_specs, out_specs=out_specs, check_vma=False)
```

time: 124 us -> 115 us (0.927); the launches traced: 122 us -> 115 us
  Pallas kernels: 117 us -> 109 us
    pallas_call x1, Pallas kernels: 117 us -> 109 us  [local(): pl.pallas_call(functools.partial(kernel, peers, heads), out_shape=(jax.Sh...]
where the time goes in v4:
time: 115 us
  Pallas kernels  109 us (95%)
  between operations  3.21 us (3%)
  local copies, waits for them, and re-layouts  1.88 us (2%)
    pallas_call x1, Pallas kernels, local(): pl.pallas_call(functools.partial(kernel, peers, heads), out_shape=(jax.Sh...  109 us

profile of v4, /device:TPU:1, one launch (start us, length us, event | category | flops | bytes accessed | tf_op | source)
XLA Modules:
  0.0 114.7 jit_solution(17955458527115738019)
XLA Ops:
  1.4 0.6 pad_maximum_fusion.scale_ref
  2.1 109.0 %shard_map.68 = (f32[18,2,1152]{2,1,0:T(2,128)}, f32[1,1]{1,0:T(1,128)}) custom-call(f32[2]{0:T(128)} %pad_maximum_fusion.scale_ref, f32[2]{0:T(128)} %bitcast.10, bf16[256,1152]{1,0:T(8,128)(2,1)} %bitcast.8, bf16[256,1152]{1,0:T(8,128)(2,1)} %bitcast.9, bf16[2,4,288,1152]{3,2,1,0:T(8,128)(2,1)} %bitcast.7), custom_call_target="tpu_custom_call" | custom-call | tf_op jit(solution)/shard_map/pallas_call | solution.py:670
  111.1 1.9 %reshape.14 = f32[18,2,4,288]{3,2,1,0:T(4,128)} reshape(f32[18,2,1152]{2,1,0:T(2,128)} %get-tuple-element.5) | data formatting | bytes 331776 | tf_op jit(solution)/shard_map/reshape | solution.py:727

commit v5 on v4

--- a/solution.py
+++ b/solution.py
@@ -104,19 +104,22 @@
         done += size
 
 
+def selection(source, columns):
+    col = iota((source.shape[0], columns), 1)
+    return (col == source).astype(F32).astype(BF)
+
+
 def pack_matrix(peers, tokens):
-    shape = (8 * peers, 3 * peers * tokens)
-    row, col = iota(shape, 0), iota(shape, 1)
+    row = iota((8 * peers, 1), 0)
     peer, inner = row // 8, row % 8
     source = (inner // tokens) * (peers * tokens) + peer * tokens + inner % tokens
-    return ((inner < 3 * tokens) & (col == source)).astype(F32).astype(BF)
+    return selection(jnp.where(inner < 3 * tokens, source, -1), 3 * peers * tokens)
 
 
 def unpack_matrix(peers, tokens, third):
-    shape = (peers * tokens, 8 * peers)
-    token, col = iota(shape, 0), iota(shape, 1)
+    token = iota((peers * tokens, 1), 0)
     source = (token // tokens) * 8 + third * tokens + token % tokens
-    return (col == source).astype(F32).astype(BF)
+    return selection(source, 8 * peers)
 
 
 def pack(rows, matrix, peers):
@@ -258,7 +261,9 @@
         self.over_y.finish()
         rows = jnp.sum(self.over_y.into[...].astype(F32), axis=0).astype(BF)
         step = self.over_z
-        step.out[...] = dot(spread, rows).reshape(step.out.shape).astype(BF)
+        planes, out_rows, lanes = step.out.shape
+        spaced = dot(spread, rows).reshape(planes, spread.shape[0] // planes, lanes)
+        step.out[...] = spaced[:, :out_rows].astype(BF)
         step.start()
         step.keep()
 
@@ -270,7 +275,7 @@
 def kernel(
     peers,
     heads,
-    scale_ref,
+    timesteps,
     ref_losses,
     latent_ref,
     noise_ref,
@@ -288,6 +293,7 @@
     attn_two,
     dout_ref,
     dqkv_ref,
+    spare_ref,
     start_pos,
     noise_pos,
     state_ref,
@@ -323,7 +329,7 @@
     half_rows = width // 2
     y_rows = half_rows // NY
     out_rows = y_rows // planes
-    z_rows = total_refs[4].shape[1]
+    z_rows = -(-out_rows // 8) * 8
 
     def at_x(index):
         return (pair, seq, index)
@@ -412,14 +418,17 @@
         )
         for use in range(2)
     ]
-    total_two, total_values, total_queries, total_keys = [
+    total_two, total_output, total_queries, total_keys, total_values = [
         Total(total_refs[7 * use : 7 * use + 7], pair, other, y, y_peers, z, z_peers)
-        for use in range(4)
+        for use in range(5)
     ]
 
     packing = pack_matrix(peers, tokens)
     unpacking = [unpack_matrix(peers, tokens, third) for third in range(3)]
-    clean_scale, noise_scale = scale_ref[0], scale_ref[1]
+    time = jnp.full((8, 128), timesteps[0, 0], jnp.int32).astype(F32)
+    plan = jnp.cos((time / 1000.0 + 0.008) / 1.008 * (math.pi / 2)) ** 2
+    clean_scale = jnp.sqrt(plan)[:1, :1]
+    noise_scale = jnp.sqrt(1.0 - plan)[:1, :1]
 
     state = clean_scale * latent_ref[...].astype(F32) + noise_scale * noise_ref[...].astype(F32)
     center = state - jnp.mean(state, axis=1, keepdims=True)
@@ -491,8 +500,10 @@
 
     for load in loads[1]:
         load.wait()
-    row, col = iota((rows, rows), 0), iota((rows, rows), 1)
-    same = (row // quarter == col // quarter) & (row % tokens == col % tokens)
+    row, col = iota((rows, 1), 0), iota((1, rows), 1)
+    row = row // quarter * tokens + row % tokens
+    col = col // quarter * tokens + col % tokens
+    same = row == col
     gathers[0].project(weights_ref[1, : 3 * LANES], qkv_two)
     attend_forward(heads, qkv_two, probs_two, attn_two, same)
     sum_start(1, attn_two, weights_ref[1, 3 * LANES :])
@@ -555,10 +566,10 @@
     swaps[1].start()
     swaps[1].keep()
 
-    shape = (planes * z_rows, y_rows)
-    row, col = iota(shape, 0), iota(shape, 1)
-    spread = (row % z_rows < out_rows) & (col == (row // z_rows) * out_rows + row % z_rows)
-    spread = spread.astype(F32).astype(BF)
+    row = iota((planes * z_rows, 1), 0)
+    inner = row % z_rows
+    source = jnp.where(inner < out_rows, (row // z_rows) * out_rows + inner, -1)
+    spread = selection(source, y_rows)
 
     total_two.start_y()
     swaps[1].finish()
@@ -582,33 +593,47 @@
     gathers[2].middle()
 
     gathers[2].project(weights_ref[0, 3 * LANES :], dout_ref)
+    for start in range(0, width, step):
+        block = dot_tn(view(2, start, step), attn_one[...])
+        store_rows(total_output.partial, start, block[:, :256], half_rows)
+        spare_ref[start : start + step, :] = pltpu.roll(block[:, 256:], 64, 1)
+    total_output.start()
+    scores_backward(heads, qkv_one, probs_one, dout_ref, dqkv_ref)
+    total_output.start_y()
     values_backward(heads, probs_one, dout_ref, dqkv_ref)
-    values = dqkv_ref[:, 2 * LANES :]
-    attn = shifted(attn_one[...], 32).astype(BF)
+    queries_keys = beside(
+        dqkv_ref[:, :LANES].astype(F32), shifted(dqkv_ref[:, LANES : 2 * LANES], 32)
+    )
+    spare = shifted(dqkv_ref[:, 2 * LANES + 256 :], 96)
+    operand = jnp.concatenate(
+        [queries_keys[:, :512], queries_keys[:, 512:] + spare], axis=1
+    ).astype(BF)
     for start in range(0, width, step):
-        block = beside(
-            dot_tn(input_one[:, start : start + step], values),
-            dot_tn(view(2, start, step), attn),
+        block = dot_tn(input_one[:, start : start + step], operand)
+        last = block[:, 512:] + spare_ref[start : start + step, :]
+        store_rows(total_queries.partial, start, block[:, :LANES], half_rows)
+        store_rows(
+            total_keys.partial,
+            start,
+            jnp.concatenate([block[:, LANES:512], last], axis=1),
+            half_rows,
         )
+    total_queries.start()
+    total_keys.start()
+    total_two.start_z(spread)
+    total_queries.start_y()
+    total_keys.start_y()
+    for start in range(0, width, step):
+        block = dot_tn(input_one[:, start : start + step], dqkv_ref[:, 2 * LANES : 2 * LANES + 256])
         store_rows(total_values.partial, start, block, half_rows)
     total_values.start()
-    total_two.start_z(spread)
     for copy in err_copies:
         copy.wait()
     err_pair[pair] = jnp.sum(err_x[...], axis=0)
     err_copy = remote(err_pair.at[pair], err_pair.at[pair], err_pair_send, err_pair_recv, other)
     err_copy.start()
     total_values.start_y()
-    scores_backward(heads, qkv_one, probs_one, dout_ref, dqkv_ref)
-    queries_keys = beside(
-        dqkv_ref[:, :LANES].astype(F32), shifted(dqkv_ref[:, LANES : 2 * LANES], 32)
-    ).astype(BF)
-    for start in range(0, width, step):
-        block = dot_tn(input_one[:, start : start + step], queries_keys)
-        store_rows(total_queries.partial, start, block[:, :LANES], half_rows)
-        store_rows(total_keys.partial, start, block[:, LANES:], half_rows)
-    total_queries.start()
-    total_keys.start()
+    total_output.start_z(spread)
     err_copy.wait()
     margin = (err_pair[0] - err_pair[1]) * (1.0 / (rows * peers * width))
     scaled = beta_dpo * (margin - (ref_losses[0] - ref_losses[1]))
@@ -616,25 +641,32 @@
     loss_out[0, 0] = loss[0, 0]
     factor = (rows * peers * beta_dpo) * jax.nn.sigmoid(scaled)
     factor = factor[:1, :1]
-    total_queries.start_y()
-    total_keys.start_y()
-    grads_out[:, 1, :] = (total_two.finish() * factor)[:out_rows]
-    total_values.start_z(spread)
     total_queries.start_z(spread)
     total_keys.start_z(spread)
-    values_output = pltpu.roll(total_values.finish(), 64, 1)
+    total_values.start_z(spread)
+    grads_out[:, 1, :] = total_two.finish() * factor
+    empty = jnp.zeros((out_rows, 128), F32)
+    output = pltpu.roll(jnp.concatenate([total_output.finish(), empty], axis=1), 96, 1)
     queries = total_queries.finish()
     keys = total_keys.finish()
+    values = pltpu.roll(jnp.concatenate([total_values.finish(), empty], axis=1), 64, 1)
+    last = keys[:, 128:]
+    lane = iota((1, 128), 1)
+    values_rest = jnp.where((lane >= 64) & (lane < 96), pltpu.roll(last, 96, 1), 0.0)
+    output_rest = jnp.where(lane >= 96, pltpu.roll(last, 32, 1), 0.0)
     grads = jnp.concatenate(
         [
             queries,
             keys[:, :128],
-            keys[:, 128:] + values_output[:, :128],
-            values_output[:, 128:],
+            jnp.where(lane < 64, last, 0.0) + values[:, :128],
+            values[:, 128:256],
+            values[:, 256:] + output[:, :128] + values_rest,
+            output[:, 128:256],
+            output[:, 256:] + output_rest,
         ],
         axis=1,
     )
-    grads_out[:, 0, :] = (grads * factor)[:out_rows]
+    grads_out[:, 0, :] = grads * factor
 
 
 def local(latents, noise, timesteps, ref_losses, weights):
@@ -646,25 +678,20 @@
     half_rows = width // 2
     y_rows = half_rows // NY
     out_rows = y_rows // planes
-    z_rows = -(-out_rows // 8) * 8
     heads = columns // HEAD_DIM
-
-    angle = (timesteps[0, 0].astype(F32) / 1000.0 + 0.008) / 1.008 * (math.pi / 2)
-    plan = jnp.cos(angle) ** 2
-    scales = jnp.stack([jnp.sqrt(plan), jnp.sqrt(1.0 - plan)])
 
     vmem = pltpu.VMEM
     dma = pltpu.SemaphoreType.DMA
     third = width // 3
     totals = []
-    for lanes in (width, 640, LANES, 256):
+    for lanes in (width, 256, LANES, 256, 256):
         totals += [
             vmem((2, half_rows, lanes), BF),
             vmem((half_rows, lanes), BF),
             vmem((NY, y_rows, lanes), BF),
             vmem((NY, y_rows, lanes), BF),
-            vmem((planes, z_rows, lanes), BF),
-            vmem((planes, z_rows, lanes), BF),
+            vmem((planes, out_rows, lanes), BF),
+            vmem((planes, out_rows, lanes), BF),
             dma((6,)),
         ]
     grads, loss = pl.pallas_call(
@@ -693,6 +720,7 @@
             vmem((rows, LANES), BF),
             vmem((rows, LANES), BF),
             vmem((rows, 3 * LANES), BF),
+            vmem((width, 128), F32),
             vmem((quarter, width), F32),
             vmem((quarter, width), F32),
             vmem((quarter, width), F32),
@@ -722,7 +750,7 @@
         compiler_params=pltpu.CompilerParams(
             collective_id=0, has_side_effects=True, vmem_limit_bytes=60 * 2**20
         ),
-    )(scales, ref_losses[:, 0], latents[0, 0], noise[0, 0], weights.transpose(1, 2, 3, 0))
+    )(timesteps, ref_losses[:, 0], latents[0, 0], noise[0, 0], weights.transpose(1, 2, 3, 0))
 
     return (loss[0, 0], grads.reshape(out_rows, 2, 4, columns))
 

time: 115 us -> 113 us (0.983)
  Pallas kernels: 109 us -> 107 us
    pallas_call x1, Pallas kernels: 109 us -> 107 us  [local(): pl.pallas_call(functools.partial(kernel, peers, heads), out_shape=(jax.Sh...]
where the time goes in v5:
time: 113 us; the launch traced here: 112 us
  Pallas kernels  107 us (95%)
  between operations  3.04 us (3%)
  local copies, waits for them, and re-layouts  1.88 us (2%)
    pallas_call x1, Pallas kernels, local(): pl.pallas_call(functools.partial(kernel, peers, heads), out_shape=(jax.Sh...  107 us

profile of v5, /device:TPU:1, one launch (start us, length us, event | category | flops | bytes accessed | tf_op | source)
XLA Modules:
  0.0 111.8 jit_solution(5648998420992022467)
XLA Ops:
  1.3 106.9 %shard_map.68 = (f32[18,2,1152]{2,1,0:T(2,128)}, f32[1,1]{1,0:T(1,128)}) custom-call(s32[1,1]{1,0:T(1,128)S(6)} %copy.8.timesteps, f32[2]{0:T(128)} %bitcast.8, bf16[256,1152]{1,0:T(8,128)(2,1)} %bitcast.6, bf16[256,1152]{1,0:T(8,128)(2,1)} %bitcast.7, bf16[2,4,288,1152]{3,2,1,0:T(8,128)(2,1)} %bitcast.5), custom_call_target="tpu_custom_call" | custom-call | tf_op jit(solution)/shard_map/pallas_call | solution.py:697
  108.2 1.9 %reshape.7 = f32[18,2,4,288]{3,2,1,0:T(4,128)} reshape(f32[18,2,1152]{2,1,0:T(2,128)} %get-tuple-element.5) | data formatting | bytes 331776 | tf_op jit(solution)/shard_map/reshape | solution.py:755

commit v6 on v5

--- a/solution.py
+++ b/solution.py
@@ -598,42 +598,44 @@
         store_rows(total_output.partial, start, block[:, :256], half_rows)
         spare_ref[start : start + step, :] = pltpu.roll(block[:, 256:], 64, 1)
     total_output.start()
+    values_backward(heads, probs_one, dout_ref, dqkv_ref)
+    for start in range(0, width, step):
+        block = dot_tn(
+            input_one[:, start : start + step], dqkv_ref[:, 2 * LANES : 2 * LANES + 256]
+        )
+        store_rows(total_values.partial, start, block, half_rows)
+    total_values.start()
+    total_output.start_y()
+    total_two.start_z(spread)
     scores_backward(heads, qkv_one, probs_one, dout_ref, dqkv_ref)
-    total_output.start_y()
-    values_backward(heads, probs_one, dout_ref, dqkv_ref)
+    total_values.start_y()
     queries_keys = beside(
         dqkv_ref[:, :LANES].astype(F32), shifted(dqkv_ref[:, LANES : 2 * LANES], 32)
     )
     spare = shifted(dqkv_ref[:, 2 * LANES + 256 :], 96)
+    operand = queries_keys[:, :LANES].astype(BF)
+    for start in range(0, width, step):
+        block = dot_tn(input_one[:, start : start + step], operand)
+        store_rows(total_queries.partial, start, block, half_rows)
+    total_queries.start()
     operand = jnp.concatenate(
-        [queries_keys[:, :512], queries_keys[:, 512:] + spare], axis=1
+        [queries_keys[:, LANES:512], queries_keys[:, 512:] + spare], axis=1
     ).astype(BF)
     for start in range(0, width, step):
         block = dot_tn(input_one[:, start : start + step], operand)
-        last = block[:, 512:] + spare_ref[start : start + step, :]
-        store_rows(total_queries.partial, start, block[:, :LANES], half_rows)
-        store_rows(
-            total_keys.partial,
-            start,
-            jnp.concatenate([block[:, LANES:512], last], axis=1),
-            half_rows,
-        )
-    total_queries.start()
+        last = block[:, 128:] + spare_ref[start : start + step, :]
+        block = jnp.concatenate([block[:, :128], last], axis=1)
+        store_rows(total_keys.partial, start, block, half_rows)
     total_keys.start()
-    total_two.start_z(spread)
     total_queries.start_y()
     total_keys.start_y()
-    for start in range(0, width, step):
-        block = dot_tn(input_one[:, start : start + step], dqkv_ref[:, 2 * LANES : 2 * LANES + 256])
-        store_rows(total_values.partial, start, block, half_rows)
-    total_values.start()
     for copy in err_copies:
         copy.wait()
     err_pair[pair] = jnp.sum(err_x[...], axis=0)
     err_copy = remote(err_pair.at[pair], err_pair.at[pair], err_pair_send, err_pair_recv, other)
     err_copy.start()
-    total_values.start_y()
     total_output.start_z(spread)
+    total_values.start_z(spread)
     err_copy.wait()
     margin = (err_pair[0] - err_pair[1]) * (1.0 / (rows * peers * width))
     scaled = beta_dpo * (margin - (ref_losses[0] - ref_losses[1]))
@@ -643,7 +645,6 @@
     factor = factor[:1, :1]
     total_queries.start_z(spread)
     total_keys.start_z(spread)
-    total_values.start_z(spread)
     grads_out[:, 1, :] = total_two.finish() * factor
     empty = jnp.zeros((out_rows, 128), F32)
     output = pltpu.roll(jnp.concatenate([total_output.finish(), empty], axis=1), 96, 1)

time: 113 us -> 112 us (level)
  no operation moved by 1% of the time
where the time goes in v6:
time: 112 us
  Pallas kernels  107 us (96%)
  between operations  3.04 us (3%)
  local copies, waits for them, and re-layouts  1.88 us (2%)
    pallas_call x1, Pallas kernels, local(): pl.pallas_call(functools.partial(kernel, peers, heads), out_shape=(jax.Sh...  107 us

profile of v6, /device:TPU:1, one launch (start us, length us, event | category | flops | bytes accessed | tf_op | source)
XLA Modules:
  0.0 111.9 jit_solution(4423911695947103353)
XLA Ops:
  1.3 107.0 %shard_map.68 = (f32[18,2,1152]{2,1,0:T(2,128)}, f32[1,1]{1,0:T(1,128)}) custom-call(s32[1,1]{1,0:T(1,128)S(6)} %copy.8.timesteps, f32[2]{0:T(128)} %bitcast.8, bf16[256,1152]{1,0:T(8,128)(2,1)} %bitcast.6, bf16[256,1152]{1,0:T(8,128)(2,1)} %bitcast.7, bf16[2,4,288,1152]{3,2,1,0:T(8,128)(2,1)} %bitcast.5), custom_call_target="tpu_custom_call" | custom-call | tf_op jit(solution)/shard_map/pallas_call | solution.py:698
  108.3 1.9 %reshape.7 = f32[18,2,4,288]{3,2,1,0:T(4,128)} reshape(f32[18,2,1152]{2,1,0:T(2,128)} %get-tuple-element.5) | data formatting | bytes 331776 | tf_op jit(solution)/shard_map/reshape | solution.py:756
